TPU v7x, 256 devices: a whole 4x4x8 slice. The times are simulated.
256 devices in a mesh: slab: 64 (over x, z, y_hi), case: 4 (over y_lo, core).
Axes of the slice: x: 4, y: 4 (y_hi: 2, y_lo: 2; y = y_hi * 2 + y_lo), z: 8, core: 2. Of those that a mesh axis runs over, the one named last changes fastest.
Arguments:
- tokens: bfloat16 [4, 128, 8, 8, 512], P('case', 'slab'), may hold values from -6 to 6
- cotangent: bfloat16 [4, 128, 8, 8, 512], P('case', 'slab'), may hold values from -6 to 6
- w_qkv: bfloat16 [512, 1536], replicated, may hold values from -4 to 4
- w_out: bfloat16 [512, 512], replicated, may hold values from -0.25 to 0.25
- w_up: bfloat16 [512, 2048], replicated, may hold values from -0.25 to 0.25
- w_down: bfloat16 [2048, 512], replicated, may hold values from -0.125 to 0.125
- gain_attn: float32 [512], replicated, may hold values from 0.1 to 1.9
- gain_mlp: float32 [512], replicated, may hold values from 0.1 to 1.9
Outputs:
- grad_tokens: bfloat16 [4, 128, 8, 8, 512], P('case', 'slab')
- grad_qkv: float32 [512, 1536], P('slab')
- grad_out: float32 [512, 512], P('slab')
- grad_up: float32 [512, 2048], P('slab')
- grad_down: float32 [2048, 512], P('slab')
- grad_gain_attn: float32 [512], P('slab')
- grad_gain_mlp: float32 [512], P('slab')
All inputs are finite; a program needn't handle non-finite values.
Results may differ from a plain program's by a relative error of at most 0.022.
Values may be sent and summed in bfloat16 or wider, within the bound.
A program may use at most 128 MiB of HBM per device.

v0:
```python
import math

import jax
import jax.numpy as jnp
from jax import lax
from jax.sharding import PartitionSpec as P

HEADS = 8


epsilon = 1e-06
root_two_pi = math.sqrt(2.0 / math.pi)


def normalize(values, gain):
    inverse = lax.rsqrt(jnp.mean(values * values, axis=-1, keepdims=True) + epsilon)
    normed = values * inverse
    return (normed, inverse, (normed * gain).astype(jnp.bfloat16))


def norm_back(grad_normed, normed, inverse, gain):
    scaled = grad_normed * gain
    return inverse * (scaled - normed * jnp.mean(scaled * normed, axis=-1, keepdims=True))


def gelu_value(inputs):
    inner = root_two_pi * (inputs + 0.044715 * inputs * inputs * inputs)
    return 0.5 * inputs * (1.0 + jnp.tanh(inner))


def gelu_slope(inputs):
    tangent = jnp.tanh(root_two_pi * (inputs + 0.044715 * inputs * inputs * inputs))
    return 0.5 * (1.0 + tangent) + 0.5 * inputs * (1.0 - tangent * tangent) * root_two_pi * (
        1.0 + 3.0 * 0.044715 * inputs * inputs
    )


def line_probs(queries, key_rows):
    scale = queries.shape[-1] ** (-0.5)
    scores = (
        jnp.einsum("blhe,bmhe->bhlm", queries, key_rows, preferred_element_type=jnp.float32) * scale
    )
    top = jnp.max(scores, axis=-1, keepdims=True)
    weights = jnp.exp(scores - top)
    return weights / jnp.sum(weights, axis=-1, keepdims=True)


def attend_lines(queries, key_rows, value_rows):
    probs = line_probs(queries, key_rows).astype(jnp.bfloat16)
    return jnp.einsum("bhlm,bmhe->blhe", probs, value_rows, preferred_element_type=jnp.float32)


def attend_back(queries, key_rows, value_rows, grad_lines):
    scale = queries.shape[-1] ** (-0.5)
    probs = line_probs(queries, key_rows)
    rounded = probs.astype(jnp.bfloat16)
    grad_values = jnp.einsum(
        "bhlm,blhe->bmhe", rounded, grad_lines, preferred_element_type=jnp.float32
    )
    grad_probs = jnp.einsum(
        "blhe,bmhe->bhlm", grad_lines, value_rows, preferred_element_type=jnp.float32
    )
    grad_scores = probs * (grad_probs - jnp.sum(probs * grad_probs, axis=-1, keepdims=True))
    score_b = grad_scores.astype(jnp.bfloat16)
    grad_queries = (
        jnp.einsum("bhlm,bmhe->blhe", score_b, key_rows, preferred_element_type=jnp.float32) * scale
    )
    grad_keys = (
        jnp.einsum("bhlm,blhe->bmhe", score_b, queries, preferred_element_type=jnp.float32) * scale
    )
    return (grad_queries, grad_keys, grad_values)


def lines_x(grid):
    return grid.reshape(grid.shape[0] * grid.shape[1], grid.shape[2], grid.shape[3], grid.shape[4])


def lines_y(grid):
    return jnp.swapaxes(grid, 1, 2).reshape(
        grid.shape[0] * grid.shape[2], grid.shape[1], grid.shape[3], grid.shape[4]
    )


def unlines_y(lines, shape):
    return jnp.swapaxes(lines.reshape(shape[0], shape[2], shape[1], shape[3], shape[4]), 1, 2)


def pencil_lines(block):
    shape = block.shape
    merged = block.reshape(shape[0], shape[1], shape[2] * 2, shape[3] // 2)
    return jnp.transpose(merged, (1, 0, 2, 3))


def pencil_block(lines, shape):
    return jnp.transpose(lines, (1, 0, 2, 3)).reshape(shape)


def body(tokens, cotangent, w_qkv, w_out, w_up, w_down, gain_attn, gain_mlp):
    depth_dev, height, across, width = tokens.shape[1:]
    count = depth_dev * height * across
    head_size = width // HEADS
    shape = (depth_dev, height, across, HEADS, head_size)
    pencil_shape = (depth_dev, height * across, HEADS // 2, 2 * head_size)
    flat = tokens.reshape(count, width).astype(jnp.float32)
    normed_one, inverse_one, hidden_one = normalize(flat, gain_attn)
    projected = jnp.dot(hidden_one, w_qkv, preferred_element_type=jnp.float32).astype(jnp.bfloat16)
    queries = projected[:, :width].reshape(shape)
    key_rows = projected[:, width : 2 * width].reshape(shape)
    value_rows = projected[:, 2 * width :].reshape(shape)
    query_block = projected[:, :width].reshape(pencil_shape)
    key_block = projected[:, width : 2 * width].reshape(pencil_shape)
    value_block = projected[:, 2 * width :].reshape(pencil_shape)
    pieces = (
        lax.all_to_all(query_block, "slab", split_axis=1, concat_axis=0, tiled=True),
        lax.all_to_all(key_block, "slab", split_axis=1, concat_axis=0, tiled=True),
        lax.all_to_all(value_block, "slab", split_axis=1, concat_axis=0, tiled=True),
    )
    line_out = attend_lines(
        pencil_lines(pieces[0]), pencil_lines(pieces[1]), pencil_lines(pieces[2])
    ).astype(jnp.bfloat16)
    out_z = lax.all_to_all(
        pencil_block(line_out, pieces[0].shape), "slab", split_axis=0, concat_axis=1, tiled=True
    )
    out_x = attend_lines(lines_x(queries), lines_x(key_rows), lines_x(value_rows)).reshape(shape)
    out_y = unlines_y(attend_lines(lines_y(queries), lines_y(key_rows), lines_y(value_rows)), shape)
    mixed = (
        (out_x + out_y + out_z.reshape(shape).astype(jnp.float32))
        .reshape(count, width)
        .astype(jnp.bfloat16)
    )
    residual = (flat + jnp.dot(mixed, w_out, preferred_element_type=jnp.float32)).astype(
        jnp.bfloat16
    )
    normed_two, inverse_two, hidden_two = normalize(residual.astype(jnp.float32), gain_mlp)
    upper = jnp.dot(hidden_two, w_up, preferred_element_type=jnp.float32)
    active = gelu_value(upper).astype(jnp.bfloat16)
    factor = 1.0 / math.sqrt(count * lax.axis_size("slab") * lax.axis_size("case"))
    grad_rows = cotangent.reshape(count, width)
    grad_active = jnp.dot(grad_rows, w_down.T, preferred_element_type=jnp.float32)
    total_down = jnp.dot(active.T, grad_rows, preferred_element_type=jnp.float32) * factor
    grad_upper = (grad_active * gelu_slope(upper)).astype(jnp.bfloat16)
    total_up = jnp.dot(hidden_two.T, grad_upper, preferred_element_type=jnp.float32) * factor
    grad_hidden_two = jnp.dot(grad_upper, w_up.T, preferred_element_type=jnp.float32)
    total_gain_two = jnp.sum(grad_hidden_two * normed_two, axis=0) * factor
    grad_residual = grad_rows.astype(jnp.float32) + norm_back(
        grad_hidden_two, normed_two, inverse_two, gain_mlp
    )
    grad_res_b = grad_residual.astype(jnp.bfloat16)
    total_out = jnp.dot(mixed.T, grad_res_b, preferred_element_type=jnp.float32) * factor
    grad_flat = jnp.dot(grad_res_b, w_out.T, preferred_element_type=jnp.float32).astype(
        jnp.bfloat16
    )
    grad_mixed = grad_flat.reshape(shape)
    grad_block = grad_flat.reshape(pencil_shape)
    pieces = (
        lax.all_to_all(query_block, "slab", split_axis=1, concat_axis=0, tiled=True),
        lax.all_to_all(key_block, "slab", split_axis=1, concat_axis=0, tiled=True),
        lax.all_to_all(value_block, "slab", split_axis=1, concat_axis=0, tiled=True),
        lax.all_to_all(grad_block, "slab", split_axis=1, concat_axis=0, tiled=True),
    )
    line_grads = attend_back(
        pencil_lines(pieces[0]),
        pencil_lines(pieces[1]),
        pencil_lines(pieces[2]),
        pencil_lines(pieces[3]),
    )
    sent_back = tuple(
        (pencil_block(piece.astype(jnp.bfloat16), pieces[0].shape) for piece in line_grads)
    )
    back_z = (
        lax.all_to_all(sent_back[0], "slab", split_axis=0, concat_axis=1, tiled=True),
        lax.all_to_all(sent_back[1], "slab", split_axis=0, concat_axis=1, tiled=True),
        lax.all_to_all(sent_back[2], "slab", split_axis=0, concat_axis=1, tiled=True),
    )
    back_x = attend_back(
        lines_x(queries), lines_x(key_rows), lines_x(value_rows), lines_x(grad_mixed)
    )
    back_y = attend_back(
        lines_y(queries), lines_y(key_rows), lines_y(value_rows), lines_y(grad_mixed)
    )
    columns = []
    for which in range(3):
        part_x = back_x[which].reshape(shape)
        part_y = unlines_y(back_y[which], shape)
        columns.append((part_x + part_y).reshape(count, width))
    grad_proj = jnp.concatenate(columns, axis=1).astype(jnp.bfloat16)
    total_qkv = jnp.dot(hidden_one.T, grad_proj, preferred_element_type=jnp.float32)
    grad_hidden_one = jnp.dot(grad_proj, w_qkv.T, preferred_element_type=jnp.float32)
    grad_proj_z = jnp.concatenate(
        [back_z[which].reshape(count, width) for which in range(3)], axis=1
    )
    total_qkv = total_qkv + jnp.dot(hidden_one.T, grad_proj_z, preferred_element_type=jnp.float32)
    grad_hidden_one = grad_hidden_one + jnp.dot(
        grad_proj_z, w_qkv.T, preferred_element_type=jnp.float32
    )
    total_qkv = total_qkv * factor
    total_gain_one = jnp.sum(grad_hidden_one * normed_one, axis=0) * factor
    grad_tokens = (
        grad_residual + norm_back(grad_hidden_one, normed_one, inverse_one, gain_attn)
    ).astype(jnp.bfloat16)
    shares = (
        lax.psum_scatter(total_qkv, "slab", scatter_dimension=0, tiled=True),
        lax.psum_scatter(total_out, "slab", scatter_dimension=0, tiled=True),
        lax.psum_scatter(total_up, "slab", scatter_dimension=0, tiled=True),
        lax.psum_scatter(total_down, "slab", scatter_dimension=0, tiled=True),
        lax.psum_scatter(total_gain_one, "slab", scatter_dimension=0, tiled=True),
        lax.psum_scatter(total_gain_two, "slab", scatter_dimension=0, tiled=True),
    )
    full_qkv, full_out, full_up, full_down, gain_one, gain_two = (
        lax.psum(shares[0].astype(jnp.bfloat16), "case").astype(jnp.float32),
        lax.psum(shares[1].astype(jnp.bfloat16), "case").astype(jnp.float32),
        lax.psum(shares[2].astype(jnp.bfloat16), "case").astype(jnp.float32),
        lax.psum(shares[3].astype(jnp.bfloat16), "case").astype(jnp.float32),
        lax.psum(shares[4].astype(jnp.bfloat16), "case").astype(jnp.float32),
        lax.psum(shares[5].astype(jnp.bfloat16), "case").astype(jnp.float32),
    )
    return (
        grad_tokens.reshape(tokens.shape),
        full_qkv,
        full_out,
        full_up,
        full_down,
        gain_one,
        gain_two,
    )


def solution(mesh):
    placed = (
        P("case", "slab", None, None, None),
        P("case", "slab", None, None, None),
        P(),
        P(),
        P(),
        P(),
        P(),
        P(),
    )
    return jax.shard_map(
        body,
        mesh=mesh,
        in_specs=placed,
        out_specs=(
            P("case", "slab", None, None, None),
            P("slab", None),
            P("slab", None),
            P("slab", None),
            P("slab", None),
            P("slab"),
            P("slab"),
        ),
        check_vma=False,
    )
```

profile of v0, /device:TPU:1, one launch (start us, length us, event | category | flops | bytes accessed | tf_op | source)
XLA Modules:
  0.0 2083.6 jit_solution(9270220634701182636)
XLA Ops:
  12.7 15.1 all-to-all-start
  28.6 10.3 all-to-all-done
  38.8 4.6 all-to-all-start.1
  44.7 9.8 all-to-all-done.1
  54.5 5.4 all-to-all-start.2
  75.5 9.5 all-to-all-start.3
  90.7 5.0 all-to-all-done.3
  129.5 7.3 all-to-all-start.4
  144.4 3.2 all-to-all-done.4
  156.7 9.1 all-to-all-start.5
  172.9 3.8 all-to-all-done.5
  176.7 8.5 all-to-all-start.6
  190.8 5.4 all-to-all-done.6
  196.2 7.0 all-to-all-start.7
  203.2 3.4 fusion.94
  210.0 4.1 all-to-all-done.7
  217.8 4.3 fusion.3
  222.2 3.8 convolution_multiply_fusion.1
  234.5 154.8 %all-reduce.2 = (bf16[512]{0:T(512)(128)(2,1)S(1)}, bf16[512]{0:T(512)(128)(2,1)S(1)}) all-reduce(f32[512]{0:T(512)S(1)} %broadcast_multiply_fusion.1, f32[512]{0:T(512)S(1)} %broadcast_multiply_fusion), channel_id=6, replica_groups=mesh['slab'=64,'case'=4] {'slab'}, use_global_device_ids=true, to_apply=%region_22.0.clone | all-reduce | flops 1024 | bytes 6144
  390.5 70.0 %reduce-scatter.7.cloned.1.call-done = f32[8,512]{1,0:T(8,128)} async-done(((f32[512,512]{1,0:T(8,128)}), f32[8,512]{1,0:T(8,128)}) %reduce-scatter.7.cloned.1.call-update) | async-done | bytes 16400 | tf_op jit(solution)/shard_map/reduce_scatter | solution.py:203
  461.9 831.3 %reduce-scatter.5.cloned.1.call-done = f32[8,1536]{1,0:T(8,128)} async-done(((f32[512,1536]{1,0:T(8,128)}), f32[8,1536]{1,0:T(8,128)}) %reduce-scatter.5.cloned.1.call-update) | async-done | bytes 49168 | tf_op jit(solution)/shard_map/reduce_scatter | solution.py:202
  1294.6 325.0 %reduce-scatter.9.cloned.1.call-done = f32[8,2048]{1,0:T(8,128)} async-done(((f32[512,2048]{1,0:T(8,128)}), f32[8,2048]{1,0:T(8,128)}) %reduce-scatter.9.cloned.1.call-update) | async-done | bytes 65552 | tf_op jit(solution)/shard_map/reduce_scatter | solution.py:204
  1621.1 358.5 %reduce-scatter.11.cloned.1.call-done = f32[32,512]{1,0:T(8,128)} async-done(((f32[2048,512]{1,0:T(8,128)}), f32[32,512]{1,0:T(8,128)}) %reduce-scatter.11.cloned.1.call-update) | async-done | bytes 65552 | tf_op jit(solution)/shard_map/reduce_scatter | solution.py:205
  1981.9 87.4 %all-reduce.6.cloned.1.call-done = (bf16[8,1536]{1,0:T(8,128)(2,1)}, bf16[8,512]{1,0:T(8,128)(2,1)}, bf16[8,2048]{1,0:T(8,128)(2,1)}, bf16[32,512]{1,0:T(8,128)(...) async-done(((bf16[8,1536]{1,0:T(8,128)(2,1)}, bf16[8,512]{1,0:T(8,128)(2,1)}, bf16[8,2048]{1,0:T(8,128)(2,1)}, bf16[32,512]{1,0:T(8,128)(2,1)}, bf16[8]{0:T(256)(128)(2,1)}, ...) | async-done | bytes 98352 | tf_op jit(solution)/shard_map/psum | solution.py:210
  (216 shorter events, 121.4 us)
Async XLA Ops:
  7.2 92.1 %copy-start = (bf16[512,2048]{1,0:T(8,128)(2,1)S(1)}, bf16[512,2048]{1,0:T(8,128)(2,1)}, u32[]{:S(2)}) copy-start(bf16[512,2048]{1,0:T(8,128)(2,1)} %param.12) | copy-start | bytes 6291460
  12.7 26.2 %all-to-all-start = ((bf16[2,64,4,128]{3,2,0,1:T(4,128)(2,1)}), bf16[2,64,4,128]{3,2,0,1:T(4,128)(2,1)S(1)}, u32[]{:S(2)}, u32[]{:S(2)}) async-start(bf16[2,64,4,128]{3,2,0,1:T(4,128)(2,1)} %copy.101), calls=%async_computation | async-start | bytes 262144 | tf_op jit(solution)/shard_map/all_to_all | solution.py:116
  38.8 23.1 %copy-start.25 = (bf16[2,64,4,128]{3,2,0,1:T(4,128)(2,1)}, bf16[2,64,4,128]{3,2,0,1:T(4,128)(2,1)S(1)}, u32[]{:S(2)}) copy-start(bf16[2,64,4,128]{3,2,0,1:T(4,128)(2,1)S(1)} %all-to-all-done) | copy-start | bytes 393220
  38.8 15.7 all-to-all-start.1
  43.7 41.3 %copy-start.15 = (bf16[16,8,8,64]{3,2,1,0:T(8,128)(2,1)}, bf16[16,8,8,64]{3,2,1,0:T(8,128)(2,1)S(1)}, u32[]{:S(2)}) copy-start(bf16[16,8,8,64]{3,2,1,0:T(8,128)(2,1)S(1)} %reshape_reshape.17) | copy-start | bytes 393220
  43.9 41.1 %copy-start.17 = (bf16[16,8,8,64]{3,2,1,0:T(8,128)(2,1)}, bf16[16,8,8,64]{3,2,1,0:T(8,128)(2,1)S(1)}, u32[]{:S(2)}) copy-start(bf16[16,8,8,64]{3,2,1,0:T(8,128)(2,1)S(1)} %reshape_reshape.16) | copy-start | bytes 393220
  54.5 16.3 all-to-all-start.2
  63.6 9.7 copy-start.22
  72.1 12.9 copy-start.30
  72.1 12.9 copy-start.36
  73.3 14.1 copy-start.44
  75.5 20.2 all-to-all-start.3
  90.7 7.9 copy-start.4
  90.7 7.9 copy-start.9
  129.5 18.2 all-to-all-start.4
  136.8 323.8 %reduce-scatter.7.cloned.1.call-start = ((), (), s32[]{:S(2)}) async-start(), calls=%async_computation.13 | async-start | bytes 1064960 | tf_op jit(solution)/shard_map/reduce_scatter | solution.py:203
  156.7 20.0 all-to-all-start.5
  176.7 19.4 all-to-all-start.6
  196.2 17.9 all-to-all-start.7
  203.2 1090.0 %reduce-scatter.5.cloned.1.call-start = ((), (), s32[]{:S(2)}) async-start(), calls=%async_computation.12 | async-start | bytes 3194880 | tf_op jit(solution)/shard_map/reduce_scatter | solution.py:202
  222.1 1397.5 %reduce-scatter.9.cloned.1.call-start = ((), (), s32[]{:S(2)}) async-start(), calls=%async_computation.14 | async-start | bytes 4259840 | tf_op jit(solution)/shard_map/reduce_scatter | solution.py:204
  226.0 1753.6 %reduce-scatter.11.cloned.1.call-start = ((), (), s32[]{:S(2)}) async-start(), calls=%async_computation.15 | async-start | bytes 4259840 | tf_op jit(solution)/shard_map/reduce_scatter | solution.py:205
  229.6 1839.7 %all-reduce.6.cloned.1.call-start = ((), (), s32[]{:S(2)}) async-start(), calls=%async_computation.16 | async-start | bytes 198656 | tf_op jit(solution)/shard_map/psum | solution.py:210
  231.5 1749.5 %copy-start.3 = (f32[128,512]{1,0:T(8,128)S(1)}, f32[128,512]{1,0:T(8,128)}, u32[]{:S(2)}) copy-start(f32[128,512]{1,0:T(8,128)} %copy-done.2) | copy-start | bytes 786436
  (36 other events, 80.4 us)
Sparse Core Ops, SparseCore 0:
  142.4 318.0 reduce-scatter.6
  467.1 826.0 reduce-scatter.4
  1295.7 323.8 reduce-scatter.8
  1622.2 357.3 reduce-scatter.10
  1983.1 86.1 all-reduce.5
where the time goes:
time: 2090 us; the launch traced here: 2080 us
  waiting for transfers between devices  1720 us (82%)
  blocking collectives  155 us (7%)
  starting transfers between devices  66.9 us (3%)
  matrix products  53.8 us (3%)
  local copies, waits for them, and re-layouts  50.5 us (2%)
  other arithmetic  25.2 us (1%)
    reduce_scatter x1, waiting for transfers between devices, body(): lax.psum_scatter(total_qkv, 'slab', scatter_dimension=0, tiled=True)  831 us
    reduce_scatter x1, waiting for transfers between devices, body(): lax.psum_scatter(total_down, 'slab', scatter_dimension=0, tiled=True)  358 us
    reduce_scatter x1, waiting for transfers between devices, body(): lax.psum_scatter(total_up, 'slab', scatter_dimension=0, tiled=True)  325 us
    unnamed x1, blocking collectives  155 us
    psum x1, waiting for transfers between devices, body(): lax.psum(shares[0].astype(jnp.bfloat16), 'case').astype(jnp.float32)  87.4 us
    reduce_scatter x1, waiting for transfers between devices, body(): lax.psum_scatter(total_out, 'slab', scatter_dimension=0, tiled=True)  70 us
  transfers between devices with their start and end apart: 13, of which 13 were waited for; matrix products, arithmetic and copies ran while one was open for 4% of the time, Pallas kernels for 0%

commit v1 on v0

--- a/solution.py
+++ b/solution.py
@@ -3,13 +3,16 @@
 import jax
 import jax.numpy as jnp
 from jax import lax
+from jax.experimental import pallas as pl
+from jax.experimental.pallas import tpu as pltpu
 from jax.sharding import PartitionSpec as P
 
 HEADS = 8
-
-
 epsilon = 1e-06
 root_two_pi = math.sqrt(2.0 / math.pi)
+MESH = pl.DeviceIdType.MESH
+F32 = jnp.float32
+BF16 = jnp.bfloat16
 
 
 def normalize(values, gain):
@@ -93,6 +96,266 @@
 
 def pencil_block(lines, shape):
     return jnp.transpose(lines, (1, 0, 2, 3)).reshape(shape)
+
+
+WIDE = 1792
+PART = 896
+
+
+def places():
+    slab, case = lax.axis_index("slab"), lax.axis_index("case")
+    return slab // 16, (slab // 2) % 8, slab % 2, case // 2, case % 2
+
+
+def device(x, z, y_hi, y_lo, core):
+    return ((x * 8 + z) * 2 + y_hi, y_lo * 2 + core)
+
+
+class Ring:
+    def __init__(self, me, dev, part, relay, fin, ss, rs):
+        self.me, self.dev, self.part, self.relay, self.fin, self.ss, self.rs = me, dev, part, relay, fin, ss, rs
+        self.right, self.left, self.over = (me + 1) % 4, (me + 3) % 4, (me + 2) % 4
+        self.copies = []
+
+    def send(self, src, dst, to):
+        n = len(self.copies)
+        copy = pltpu.make_async_remote_copy(
+            src_ref=src,
+            dst_ref=dst,
+            send_sem=self.ss.at[n],
+            recv_sem=self.rs.at[n],
+            device_id=self.dev(to),
+            device_id_type=MESH,
+        )
+        copy.start()
+        self.copies.append(copy)
+
+    def start(self):
+        self.send(self.part(self.over, 0), self.relay.at[0], self.right)
+        self.send(self.part(self.over, 1), self.relay.at[1], self.left)
+        self.send(self.part(self.right, 1), self.fin.at[1], self.right)
+        self.send(self.part(self.left, 0), self.fin.at[2], self.left)
+
+    def middle(self):
+        for h, to, slot in ((0, self.right, 0), (1, self.left, 3)):
+            self.copies[h].wait_recv()
+            ref = self.part(to, h)
+            ref[...] = (ref[...].astype(F32) + self.relay[h].astype(F32)).astype(BF16)
+            self.send(ref, self.fin.at[slot], to)
+
+    def finish(self):
+        for copy in self.copies[2:]:
+            copy.wait_recv()
+
+    def result(self, h):
+        a, b = (0, 2) if h == 0 else (1, 3)
+        own = self.part(self.me, h)[...].astype(F32)
+        return (own + self.fin[a].astype(F32) + self.fin[b].astype(F32)).astype(BF16)
+
+    def drain(self):
+        for copy in self.copies:
+            copy.wait_send()
+
+
+def reduce_kernel(
+    factor,
+    h1, gp, mixed, grb, h2, gu, act, cot, gains,
+    o_qkv, o_out, o_up, o_down, o_g1, o_g2,
+    b_h1, b_gp, b_mixed, b_grb, b_h2, b_gu, b_act, b_cot,
+    down32, buf, relay_a, fin_a, relay_b, fin_b, a1, b1, relay_a2, fin_a2, relay_b2, fin_b2,
+    zbuf, zrecv, gath,
+    ss_core, rs_core, ss_ring, rs_ring, ss_z, rs_z, ss_g, rs_g,
+):
+    x, z, y_hi, y_lo, core = places()
+    y = y_hi * 2 + y_lo
+    barrier = pltpu.get_barrier_semaphore()
+    peers = [
+        device(x, z, y_hi, y_lo, 1 - core),
+        device(x, z, y_hi, 1 - y_lo, core),
+        device(x, z, y_hi, 1 - y_lo, 1 - core),
+        device(x, z, 1 - y_hi, 1 - y_lo, core),
+        device((x + 1) % 4, z, y_hi, y_lo, core),
+        device((x + 3) % 4, z, y_hi, y_lo, core),
+    ] + [device(x, (z + d) % 8, y_hi, y_lo, core) for d in range(1, 8)]
+    for peer in peers:
+        pl.semaphore_signal(barrier, inc=1, device_id=peer, device_id_type=MESH)
+    pl.semaphore_wait(barrier, len(peers))
+
+    other = device(x, z, y_hi, y_lo, 1 - core)
+    wide = ((h2, b_h2, 0), (gu, b_gu, 1024), (act, b_act, 0), (cot, b_cot, 256), (mixed, b_mixed, 0),
+            (grb, b_grb, 256), (h1, b_h1, 0), (gp, b_gp, 768))
+    core_copies = []
+    for n, (src, dst, half) in enumerate(wide):
+        if half:
+            there = src.at[:, pl.ds(pl.multiple_of((1 - core) * half, 128), half)]
+        else:
+            there = src
+        copy = pltpu.make_async_remote_copy(
+            src_ref=there,
+            dst_ref=dst.at[pl.ds(128, 128)],
+            send_sem=ss_core.at[n],
+            recv_sem=rs_core.at[n],
+            device_id=other,
+            device_id_type=MESH,
+        )
+        copy.start()
+        core_copies.append(copy)
+    for src, dst, half in wide:
+        if half:
+            dst[0:128, :] = src[:, pl.ds(pl.multiple_of(core * half, 128), half)]
+        else:
+            dst[0:128, :] = src[...]
+    for copy in core_copies:
+        copy.wait_recv()
+
+    def product(a, b):
+        return lax.dot_general(a, b, (((0,), (0,)), ((), ())), preferred_element_type=F32)
+
+    def put(at, upper, lower):
+        width = upper.shape[-1]
+        both = jnp.concatenate([upper, lower], axis=1).astype(BF16)
+        buf[:, :, :, :, at : at + width] = both.reshape(4, 8, 2, 16, width)
+
+    down32[...] = product(b_act[...], b_cot[...]).reshape(64, 32, 256)
+    for i in range(4):
+        lower = product(b_h2[...], b_gu[:, 256 * i : 256 * i + 256]).reshape(64, 8, 256)
+        if i < 3:
+            upper = product(b_h1[...], b_gp[:, 256 * i : 256 * i + 256]).reshape(64, 8, 256)
+        else:
+            upper = product(b_mixed[...], b_grb[...]).reshape(64, 8, 256)
+        put(256 * i if i < 3 else PART, upper, lower)
+    put(PART + 256, down32[:, 0:8, :], down32[:, 16:24, :])
+    put(PART + 512, down32[:, 8:16, :], down32[:, 24:32, :])
+    buf[:, :, :, :, 768:PART] = gains[...].reshape(4, 8, 2, 16, 128)
+    buf[:, :, :, :, WIDE - 128 : WIDE] = jnp.zeros((4, 8, 2, 16, 128), BF16)
+
+    def lanes(lo):
+        return pl.ds(pl.multiple_of(lo * PART, 128), PART)
+
+    def dev_x(i):
+        return device(i, z, y_hi, y_lo, core)
+
+    def dev_y(i):
+        return device(x, z, i // 2, i % 2, core)
+
+    def dev_z(i):
+        return device(x, i, y_hi, y_lo, core)
+
+    ring_a = Ring(x, dev_x, lambda i, h: buf.at[i, pl.ds(2 * h, 2)], relay_a, fin_a, ss_ring.at[0], rs_ring.at[0])
+    ring_b = Ring(
+        y, dev_y, lambda i, h: buf.at[pl.ds(2 * h, 2), pl.ds(4, 4), i // 2, :, lanes(i % 2)],
+        relay_b, fin_b, ss_ring.at[1], rs_ring.at[1],
+    )
+    ring_a2 = Ring(
+        y, dev_y, lambda i, h: a1.at[pl.ds(2 * h, 2), i // 2, :, lanes(i % 2)],
+        relay_a2, fin_a2, ss_ring.at[2], rs_ring.at[2],
+    )
+    ring_b2 = Ring(x, dev_x, lambda i, h: b1.at[i, pl.ds(2 * h, 2)], relay_b2, fin_b2, ss_ring.at[3], rs_ring.at[3])
+    ring_a.start()
+    ring_b.start()
+    ring_a.middle()
+    ring_b.middle()
+    ring_a.finish()
+    for h in range(2):
+        a1[2 * h : 2 * h + 2] = ring_a.result(h)
+    ring_a2.start()
+    ring_b.finish()
+    for h in range(2):
+        b1[2 * h : 2 * h + 2] = ring_b.result(h)
+    ring_b2.start()
+    ring_a2.middle()
+    ring_b2.middle()
+    ring_a2.finish()
+    for h in range(2):
+        zbuf[2 * h : 2 * h + 2] = ring_a2.result(h)
+    ring_b2.finish()
+    for h in range(2):
+        zbuf[4 + 2 * h : 6 + 2 * h] = ring_b2.result(h)
+    z_copies = []
+    for d in range(1, 8):
+        to = (z + d) % 8
+        copy = pltpu.make_async_remote_copy(
+            src_ref=zbuf.at[to],
+            dst_ref=zrecv.at[d - 1],
+            send_sem=ss_z.at[d - 1],
+            recv_sem=rs_z.at[d - 1],
+            device_id=dev_z(to),
+            device_id_type=MESH,
+        )
+        copy.start()
+        z_copies.append(copy)
+    total = zbuf[z].astype(F32)
+    for d in range(7):
+        z_copies[d].wait_recv()
+        total = total + zrecv[d].astype(F32)
+    mine = y_lo * 2 + core
+    gath[mine] = total.astype(BF16)
+    g_copies = []
+    for n, (dy, dc) in enumerate(((0, 1), (1, 0), (1, 1))):
+        yl, co = (y_lo + dy) % 2, (core + dc) % 2
+        copy = pltpu.make_async_remote_copy(
+            src_ref=gath.at[mine],
+            dst_ref=gath.at[mine],
+            send_sem=ss_g.at[n],
+            recv_sem=rs_g.at[n],
+            device_id=device(x, z, y_hi, yl, co),
+            device_id_type=MESH,
+        )
+        copy.start()
+        g_copies.append(copy)
+    for copy in g_copies:
+        copy.wait_recv()
+    g1 = jnp.zeros((8, 128), F32)
+    g2 = jnp.zeros((8, 128), F32)
+    for c in range(2):
+        low = gath[c].astype(F32) * factor
+        high = gath[2 + c].astype(F32) * factor
+        o_qkv[:, 768 * c : 768 * c + 768] = low[0:8, 0:768]
+        o_out[:, 256 * c : 256 * c + 256] = high[0:8, 0:256]
+        o_up[:, 1024 * c : 1024 * c + 768] = low[8:16, 0:768]
+        o_up[:, 1024 * c + 768 : 1024 * c + 1024] = high[8:16, 0:256]
+        at = slice(256 * c, 256 * c + 256)
+        o_down[0:8, at] = high[0:8, 256:512]
+        o_down[8:16, at] = high[0:8, 512:768]
+        o_down[16:24, at] = high[8:16, 256:512]
+        o_down[24:32, at] = high[8:16, 512:768]
+        g1 = g1 + low[0:8, 768:PART]
+        g2 = g2 + low[8:16, 768:PART]
+    o_g1[...] = g1
+    o_g2[...] = g2
+    for copy in core_copies + z_copies + g_copies:
+        copy.wait_send()
+    for ring in (ring_a, ring_b, ring_a2, ring_b2):
+        ring.drain()
+
+
+def reduce_weights(factor, *arrays):
+    vm = pltpu.VMEM
+    dma = pltpu.SemaphoreType.DMA
+    shapes = ((8, 1536), (8, 512), (8, 2048), (32, 512), (8, 128), (8, 128))
+    return pl.pallas_call(
+        lambda *refs: reduce_kernel(factor, *refs),
+        out_shape=[jax.ShapeDtypeStruct(s, F32) for s in shapes],
+        in_specs=[pl.BlockSpec(memory_space=vm)] * 9,
+        out_specs=[pl.BlockSpec(memory_space=vm)] * 6,
+        scratch_shapes=[
+            vm((256, 512), BF16), vm((256, 768), BF16), vm((256, 512), BF16), vm((256, 256), BF16),
+            vm((256, 512), BF16), vm((256, 1024), BF16), vm((256, 2048), BF16), vm((256, 256), BF16),
+            vm((64, 32, 256), F32),
+            vm((4, 8, 2, 16, WIDE), BF16),
+            vm((2, 2, 2, 16, WIDE), BF16), vm((4, 2, 2, 16, WIDE), BF16),
+            vm((2, 2, 4, 16, PART), BF16), vm((4, 2, 4, 16, PART), BF16),
+            vm((4, 2, 16, WIDE), BF16), vm((4, 4, 16, PART), BF16),
+            vm((2, 2, 16, PART), BF16), vm((4, 2, 16, PART), BF16),
+            vm((2, 2, 16, PART), BF16), vm((4, 2, 16, PART), BF16),
+            vm((8, 16, PART), BF16), vm((7, 16, PART), BF16), vm((4, 16, PART), BF16),
+            dma((8,)), dma((8,)), dma((4, 6)), dma((4, 6)), dma((7,)), dma((7,)), dma((3,)), dma((3,)),
+        ],
+        compiler_params=pltpu.CompilerParams(
+            collective_id=1, has_side_effects=True, vmem_limit_bytes=40 * 1024 * 1024
+        ),
+        cost_estimate=pl.CostEstimate(flops=800_000_000, bytes_accessed=4_000_000, transcendentals=0),
+    )(*arrays)
 
 
 def body(tokens, cotangent, w_qkv, w_out, w_up, w_down, gain_attn, gain_mlp):
@@ -137,25 +400,19 @@
     factor = 1.0 / math.sqrt(count * lax.axis_size("slab") * lax.axis_size("case"))
     grad_rows = cotangent.reshape(count, width)
     grad_active = jnp.dot(grad_rows, w_down.T, preferred_element_type=jnp.float32)
-    total_down = jnp.dot(active.T, grad_rows, preferred_element_type=jnp.float32) * factor
     grad_upper = (grad_active * gelu_slope(upper)).astype(jnp.bfloat16)
-    total_up = jnp.dot(hidden_two.T, grad_upper, preferred_element_type=jnp.float32) * factor
     grad_hidden_two = jnp.dot(grad_upper, w_up.T, preferred_element_type=jnp.float32)
-    total_gain_two = jnp.sum(grad_hidden_two * normed_two, axis=0) * factor
+    total_gain_two = jnp.sum(grad_hidden_two * normed_two, axis=0)
     grad_residual = grad_rows.astype(jnp.float32) + norm_back(
         grad_hidden_two, normed_two, inverse_two, gain_mlp
     )
     grad_res_b = grad_residual.astype(jnp.bfloat16)
-    total_out = jnp.dot(mixed.T, grad_res_b, preferred_element_type=jnp.float32) * factor
     grad_flat = jnp.dot(grad_res_b, w_out.T, preferred_element_type=jnp.float32).astype(
         jnp.bfloat16
     )
     grad_mixed = grad_flat.reshape(shape)
     grad_block = grad_flat.reshape(pencil_shape)
-    pieces = (
-        lax.all_to_all(query_block, "slab", split_axis=1, concat_axis=0, tiled=True),
-        lax.all_to_all(key_block, "slab", split_axis=1, concat_axis=0, tiled=True),
-        lax.all_to_all(value_block, "slab", split_axis=1, concat_axis=0, tiled=True),
+    pieces = pieces + (
         lax.all_to_all(grad_block, "slab", split_axis=1, concat_axis=0, tiled=True),
     )
     line_grads = attend_back(
@@ -182,46 +439,31 @@
     for which in range(3):
         part_x = back_x[which].reshape(shape)
         part_y = unlines_y(back_y[which], shape)
-        columns.append((part_x + part_y).reshape(count, width))
+        columns.append(
+            (part_x + part_y).reshape(count, width)
+            + back_z[which].reshape(count, width).astype(jnp.float32)
+        )
     grad_proj = jnp.concatenate(columns, axis=1).astype(jnp.bfloat16)
-    total_qkv = jnp.dot(hidden_one.T, grad_proj, preferred_element_type=jnp.float32)
     grad_hidden_one = jnp.dot(grad_proj, w_qkv.T, preferred_element_type=jnp.float32)
-    grad_proj_z = jnp.concatenate(
-        [back_z[which].reshape(count, width) for which in range(3)], axis=1
-    )
-    total_qkv = total_qkv + jnp.dot(hidden_one.T, grad_proj_z, preferred_element_type=jnp.float32)
-    grad_hidden_one = grad_hidden_one + jnp.dot(
-        grad_proj_z, w_qkv.T, preferred_element_type=jnp.float32
-    )
-    total_qkv = total_qkv * factor
-    total_gain_one = jnp.sum(grad_hidden_one * normed_one, axis=0) * factor
+    total_gain_one = jnp.sum(grad_hidden_one * normed_one, axis=0)
     grad_tokens = (
         grad_residual + norm_back(grad_hidden_one, normed_one, inverse_one, gain_attn)
     ).astype(jnp.bfloat16)
-    shares = (
-        lax.psum_scatter(total_qkv, "slab", scatter_dimension=0, tiled=True),
-        lax.psum_scatter(total_out, "slab", scatter_dimension=0, tiled=True),
-        lax.psum_scatter(total_up, "slab", scatter_dimension=0, tiled=True),
-        lax.psum_scatter(total_down, "slab", scatter_dimension=0, tiled=True),
-        lax.psum_scatter(total_gain_one, "slab", scatter_dimension=0, tiled=True),
-        lax.psum_scatter(total_gain_two, "slab", scatter_dimension=0, tiled=True),
-    )
-    full_qkv, full_out, full_up, full_down, gain_one, gain_two = (
-        lax.psum(shares[0].astype(jnp.bfloat16), "case").astype(jnp.float32),
-        lax.psum(shares[1].astype(jnp.bfloat16), "case").astype(jnp.float32),
-        lax.psum(shares[2].astype(jnp.bfloat16), "case").astype(jnp.float32),
-        lax.psum(shares[3].astype(jnp.bfloat16), "case").astype(jnp.float32),
-        lax.psum(shares[4].astype(jnp.bfloat16), "case").astype(jnp.float32),
-        lax.psum(shares[5].astype(jnp.bfloat16), "case").astype(jnp.float32),
+    gains = jnp.concatenate(
+        [total_gain_one.reshape(64, 8, 1), total_gain_two.reshape(64, 8, 1)], axis=1
+    )
+    gains = jnp.broadcast_to(gains, (64, 16, 128)).astype(jnp.bfloat16)
+    sums = reduce_weights(
+        factor, hidden_one, grad_proj, mixed, grad_res_b, hidden_two, grad_upper, active, grad_rows, gains
     )
     return (
         grad_tokens.reshape(tokens.shape),
-        full_qkv,
-        full_out,
-        full_up,
-        full_down,
-        gain_one,
-        gain_two,
+        sums[0],
+        sums[1],
+        sums[2],
+        sums[3],
+        sums[4][:, 0],
+        sums[5][:, 0],
     )
 
 

time: 2090 us -> 265 us (0.13)
  waiting for transfers between devices: 1720 us -> 40.9 us
  blocking collectives: 155 us -> 0 us
  Pallas kernels: 0 us -> 50.3 us
    reduce_scatter x4 -> x0, waiting for transfers between devices: 1580 us -> none  [the longest x1 831 us: body(): lax.psum_scatter(total_qkv, 'slab', scatter_dimension=0, tiled=True)]
    unnamed x1 -> x0, blocking collectives: 155 us -> none
    psum x1 -> x0, waiting for transfers between devices: 87.4 us -> none  [body(): lax.psum(shares[0].astype(jnp.bfloat16), 'case').astype(jnp.float32)]
    pallas_call x0 -> x1, Pallas kernels: none -> 50.3 us  [reduce_weights(): pl.pallas_call(lambda *refs: reduce_kernel(factor, *refs), out_shape=[jax...]
  transfers between devices with their start and end apart: 13 -> 8, of which waited for: 13 -> 8; matrix products, arithmetic and copies ran while one was open for 4% -> 17% of each run, Pallas kernels for 0% -> 0%
where the time goes in v1:
time: 265 us; the launch traced here: 264 us
  starting transfers between devices  68.3 us (26%)
  Pallas kernels  50.3 us (19%)
  local copies, waits for them, and re-layouts  48.2 us (18%)
  waiting for transfers between devices  40.9 us (15%)
  matrix products  37.8 us (14%)
  other arithmetic  16.7 us (6%)
    pallas_call x1, Pallas kernels, reduce_weights(): pl.pallas_call(lambda *refs: reduce_kernel(factor, *refs), out_shape=[jax...  50.3 us
    all_to_all x1, starting transfers between devices, body(): lax.all_to_all(query_block, 'slab', split_axis=1, concat_axis=0, tiled=True)  15.1 us
    all_to_all x1, starting transfers between devices, body(): lax.all_to_all(pencil_block(line_out, pieces[0].shape), 'slab', split_axi...  11.1 us
    all_to_all x1, starting transfers between devices, body(): lax.all_to_all(sent_back[2], 'slab', split_axis=0, concat_axis=1, tiled=T...  11 us
    unnamed x108, local copies, waits for them, and re-layouts  11 us
    all_to_all x1, waiting for transfers between devices, body(): lax.all_to_all(query_block, 'slab', split_axis=1, concat_axis=0, tiled=True)  10.3 us
    all_to_all x1, waiting for transfers between devices, body(): lax.all_to_all(key_block, 'slab', split_axis=1, concat_axis=0, tiled=True)  9.36 us
    all_to_all x1, starting transfers between devices, body(): lax.all_to_all(sent_back[1], 'slab', split_axis=0, concat_axis=1, tiled=T...  7.49 us
  transfers between devices with their start and end apart: 8, of which 8 were waited for; matrix products, arithmetic and copies ran while one was open for 17% of the time, Pallas kernels for 0%

profile of v1, /device:TPU:1, one launch (start us, length us, event | category | flops | bytes accessed | tf_op | source)
XLA Modules:
  0.0 263.6 jit_solution(7646574330856490277)
XLA Ops:
  5.5 15.1 %all-to-all-start.1 = ((bf16[2,64,4,128]{3,2,0,1:T(4,128)(2,1)}), bf16[2,64,4,128]{3,2,0,1:T(4,128)(2,1)S(1)}, u32[]{:S(2)}, u32[]{:S(2)}) async-start(bf16[2,64,4,128]{3,2,0,1:T(4,128)(2,1)} %copy.154), calls=%async_computation.1 | async-start | bytes 262144 | tf_op jit(solution)/shard_map/all_to_all | solution.py:377
  21.4 10.3 %all-to-all-done.1 = bf16[2,64,4,128]{3,2,0,1:T(4,128)(2,1)S(1)} async-done(((bf16[2,64,4,128]{3,2,0,1:T(4,128)(2,1)}), bf16[2,64,4,128]{3,2,0,1:T(4,128)(2,1)S(1)}, u32[]{:S(2)}, u32[]{:S(2)}) %all-to-all-start.1) | async-done | bytes 131104 | tf_op jit(solution)/shard_map/all_to_all | solution.py:377
  31.7 5.5 %all-to-all-start.2 = ((bf16[2,64,4,128]{3,2,0,1:T(4,128)(2,1)}), bf16[2,64,4,128]{3,2,0,1:T(4,128)(2,1)}, u32[]{:S(2)}, u32[]{:S(2)}) async-start(bf16[2,64,4,128]{3,2,0,1:T(4,128)(2,1)} %copy.155), calls=%async_computation.2 | async-start | bytes 262144 | tf_op jit(solution)/shard_map/all_to_all | solution.py:378
  38.6 9.4 %all-to-all-done.2 = bf16[2,64,4,128]{3,2,0,1:T(4,128)(2,1)} async-done(((bf16[2,64,4,128]{3,2,0,1:T(4,128)(2,1)}), bf16[2,64,4,128]{3,2,0,1:T(4,128)(2,1)}, u32[]{:S(2)}, u32[]{:S(2)}) %all-to-all-start.2) | async-done | bytes 131104 | tf_op jit(solution)/shard_map/all_to_all | solution.py:378
  48.0 5.5 %all-to-all-start = ((bf16[2,64,4,128]{3,2,0,1:T(4,128)(2,1)}), bf16[2,64,4,128]{3,2,0,1:T(4,128)(2,1)}, u32[]{:S(2)}, u32[]{:S(2)}) async-start(bf16[2,64,4,128]{3,2,0,1:T(4,128)(2,1)} %copy.153), calls=%async_computation | async-start | bytes 262144 | tf_op jit(solution)/shard_map/all_to_all | solution.py:379
  58.3 2.9 %fusion.77 = (f32[16,8,8]{2,1,0:T(8,128)}, f32[16,8,8,8]{2,3,1,0:T(8,128)}) fusion(bf16[16,8,8,64]{3,2,1,0:T(8,128)(2,1)} %reshape_reshape.17, bf16[16,8,8,64]{3,2,1,0:T(8,128)(2,1)} %reshape_reshape.16), kind=kOutput, calls=%fused_computation.106 | convolution fusion | flops 1073159 | bytes 299008 | tf_op jit(solution)/shard_map/sub | solution.py:47
  69.7 11.1 %all-to-all-start.3 = ((bf16[128,1,4,128]{3,2,1,0:T(4,128)(2,1)}), bf16[128,1,4,128]{3,2,1,0:T(4,128)(2,1)}, u32[]{:S(2)}, u32[]{:S(2)}) async-start(bf16[128,1,4,128]{3,2,1,0:T(4,128)(2,1)} %copy.160), calls=%async_computation.3 | async-start | bytes 262144 | tf_op jit(solution)/shard_map/all_to_all | solution.py:384
  80.8 2.4 fusion.39
  84.1 2.3 fusion.29
  86.3 5.2 %all-to-all-done.3 = bf16[128,1,4,128]{3,2,1,0:T(4,128)(2,1)} async-done(((bf16[128,1,4,128]{3,2,1,0:T(4,128)(2,1)}), bf16[128,1,4,128]{3,2,1,0:T(4,128)(2,1)}, u32[]{:S(2)}, u32[]{:S(2)}) %all-to-all-start.3) | async-done | bytes 131104 | tf_op jit(solution)/shard_map/all_to_all | solution.py:384
  94.4 2.1 fusion.20
  116.0 6.8 %all-to-all-start.4 = ((bf16[2,64,4,128]{3,2,0,1:T(4,128)(2,1)}), bf16[2,64,4,128]{3,2,0,1:T(4,128)(2,1)S(1)}, u32[]{:S(2)}, u32[]{:S(2)}) async-start(bf16[2,64,4,128]{3,2,0,1:T(4,128)(2,1)} %copy.171), calls=%async_computation.4 | async-start | bytes 262144 | tf_op jit(solution)/shard_map/all_to_all | solution.py:416
  122.8 2.2 bitcast_add_fusion.2
  125.1 2.2 bitcast_add_fusion.1
  127.2 6.7 %all-to-all-done.4 = bf16[2,64,4,128]{3,2,0,1:T(4,128)(2,1)S(1)} async-done(((bf16[2,64,4,128]{3,2,0,1:T(4,128)(2,1)}), bf16[2,64,4,128]{3,2,0,1:T(4,128)(2,1)S(1)}, u32[]{:S(2)}, u32[]{:S(2)}) %all-to-all-start.4) | async-done | bytes 131104 | tf_op jit(solution)/shard_map/all_to_all | solution.py:416
  140.6 5.8 %all-to-all-start.5 = ((bf16[128,1,4,128]{3,2,1,0:T(4,128)(2,1)}), bf16[128,1,4,128]{3,2,1,0:T(4,128)(2,1)}, u32[]{:S(2)}, u32[]{:S(2)}) async-start(bf16[128,1,4,128]{3,2,1,0:T(4,128)(2,1)} %copy.176), calls=%async_computation.5 | async-start | bytes 262144 | tf_op jit(solution)/shard_map/all_to_all | solution.py:428
  146.4 2.4 fusion.37
  152.4 4.9 %all-to-all-done.5 = bf16[128,1,4,128]{3,2,1,0:T(4,128)(2,1)} async-done(((bf16[128,1,4,128]{3,2,1,0:T(4,128)(2,1)}), bf16[128,1,4,128]{3,2,1,0:T(4,128)(2,1)}, u32[]{:S(2)}, u32[]{:S(2)}) %all-to-all-start.5) | async-done | bytes 131104 | tf_op jit(solution)/shard_map/all_to_all | solution.py:428
  157.2 7.5 %all-to-all-start.6 = ((bf16[128,1,4,128]{3,2,1,0:T(4,128)(2,1)}), bf16[128,1,4,128]{3,2,1,0:T(4,128)(2,1)}, u32[]{:S(2)}, u32[]{:S(2)}) async-start(bf16[128,1,4,128]{3,2,1,0:T(4,128)(2,1)} %copy.184), calls=%async_computation.6 | async-start | bytes 262144 | tf_op jit(solution)/shard_map/all_to_all | solution.py:429
  164.7 2.5 fusion.24
  170.3 2.3 convolution_convert_fusion.1
  175.6 11.0 %all-to-all-start.7 = ((bf16[128,1,4,128]{3,2,1,0:T(4,128)(2,1)}), bf16[128,1,4,128]{3,2,1,0:T(4,128)(2,1)}, u32[]{:S(2)}, u32[]{:S(2)}) async-start(bf16[128,1,4,128]{3,2,1,0:T(4,128)(2,1)} %copy.192), calls=%async_computation.7 | async-start | bytes 262144 | tf_op jit(solution)/shard_map/all_to_all | solution.py:430
  186.6 2.2 bitcast_add_fusion
  208.6 50.3 %shard_map.135 = (f32[8,1536]{1,0:T(8,128)S(1)}, f32[8,512]{1,0:T(8,128)S(1)}, f32[8,2048]{1,0:T(8,128)S(1)}, f32[32,512]{1,0:T(8,128)S(1)}, f32[8,128]{1,0:T(8,128)S(1)}, /*index=5*/f32[8,128]{1,0:T(8,128)S(1)}) custom-call(bf16[128,512]{1,0:T(8,128)(2,1)S(1)} %multiply_convert_fusion.5.refs_0_, bf16[128,1536]{1,0:T(8,128)(2,1)S(1)} %pad_maximum_fusion.refs_1_, ...), custom_call_target="tpu_custom_call" | custom-call | flops 800000000 | bytes 4000000 | tf_op jit(solution)/shard_map/pallas_call | solution.py:336
  (197 shorter events, 83.8 us)
Async XLA Ops:
  0.6 97.6 %copy-start = (bf16[512,2048]{1,0:T(8,128)(2,1)S(1)}, bf16[512,2048]{1,0:T(8,128)(2,1)}, u32[]{:S(2)}) copy-start(bf16[512,2048]{1,0:T(8,128)(2,1)} %param.12) | copy-start | bytes 6291460
  5.5 26.2 %all-to-all-start.1 = ((bf16[2,64,4,128]{3,2,0,1:T(4,128)(2,1)}), bf16[2,64,4,128]{3,2,0,1:T(4,128)(2,1)S(1)}, u32[]{:S(2)}, u32[]{:S(2)}) async-start(bf16[2,64,4,128]{3,2,0,1:T(4,128)(2,1)} %copy.154), calls=%async_computation.1 | async-start | bytes 262144 | tf_op jit(solution)/shard_map/all_to_all | solution.py:377
  31.7 16.3 %all-to-all-start.2 = ((bf16[2,64,4,128]{3,2,0,1:T(4,128)(2,1)}), bf16[2,64,4,128]{3,2,0,1:T(4,128)(2,1)}, u32[]{:S(2)}, u32[]{:S(2)}) async-start(bf16[2,64,4,128]{3,2,0,1:T(4,128)(2,1)} %copy.155), calls=%async_computation.2 | async-start | bytes 262144 | tf_op jit(solution)/shard_map/all_to_all | solution.py:378
  37.7 43.1 %copy-start.14 = (bf16[2,8,8,8,64]{4,2,3,1,0:T(8,128)(2,1)}, bf16[2,8,8,8,64]{4,2,3,1,0:T(8,128)(2,1)S(1)}, u32[]{:S(2)}) copy-start(bf16[2,8,8,8,64]{4,2,3,1,0:T(8,128)(2,1)S(1)} %copy.148) | copy-start | bytes 393220
  37.9 42.9 %copy-start.16 = (bf16[2,8,8,8,64]{4,2,3,1,0:T(8,128)(2,1)}, bf16[2,8,8,8,64]{4,2,3,1,0:T(8,128)(2,1)S(1)}, u32[]{:S(2)}) copy-start(bf16[2,8,8,8,64]{4,2,3,1,0:T(8,128)(2,1)S(1)} %copy.149) | copy-start | bytes 393220
  48.0 16.3 %all-to-all-start = ((bf16[2,64,4,128]{3,2,0,1:T(4,128)(2,1)}), bf16[2,64,4,128]{3,2,0,1:T(4,128)(2,1)}, u32[]{:S(2)}, u32[]{:S(2)}) async-start(bf16[2,64,4,128]{3,2,0,1:T(4,128)(2,1)} %copy.153), calls=%async_computation | async-start | bytes 262144 | tf_op jit(solution)/shard_map/all_to_all | solution.py:379
  65.6 17.6 %copy-start.35 = (bf16[128,8,64]{0,2,1:T(8,128)(2,1)}, bf16[128,8,64]{0,2,1:T(8,128)(2,1)S(1)}, u32[]{:S(2)}) copy-start(bf16[128,8,64]{0,2,1:T(8,128)(2,1)S(1)} %copy.158) | copy-start | bytes 393220
  67.9 16.2 %copy-start.18 = (bf16[16,8,8,64]{3,2,1,0:T(8,128)(2,1)S(1)}, bf16[16,8,8,64]{3,2,1,0:T(8,128)(2,1)}, u32[]{:S(2)}) copy-start(bf16[16,8,8,64]{3,2,1,0:T(8,128)(2,1)} %reshape_reshape.16) | copy-start | bytes 393220
  67.9 16.2 %copy-start.20 = (bf16[16,8,8,64]{3,2,1,0:T(8,128)(2,1)S(1)}, bf16[16,8,8,64]{3,2,1,0:T(8,128)(2,1)}, u32[]{:S(2)}) copy-start(bf16[16,8,8,64]{3,2,1,0:T(8,128)(2,1)} %reshape_reshape.17) | copy-start | bytes 393220
  69.7 21.8 %all-to-all-start.3 = ((bf16[128,1,4,128]{3,2,1,0:T(4,128)(2,1)}), bf16[128,1,4,128]{3,2,1,0:T(4,128)(2,1)}, u32[]{:S(2)}, u32[]{:S(2)}) async-start(bf16[128,1,4,128]{3,2,1,0:T(4,128)(2,1)} %copy.160), calls=%async_computation.3 | async-start | bytes 262144 | tf_op jit(solution)/shard_map/all_to_all | solution.py:384
  116.0 17.9 %all-to-all-start.4 = ((bf16[2,64,4,128]{3,2,0,1:T(4,128)(2,1)}), bf16[2,64,4,128]{3,2,0,1:T(4,128)(2,1)S(1)}, u32[]{:S(2)}, u32[]{:S(2)}) async-start(bf16[2,64,4,128]{3,2,0,1:T(4,128)(2,1)} %copy.171), calls=%async_computation.4 | async-start | bytes 262144 | tf_op jit(solution)/shard_map/all_to_all | solution.py:416
  140.6 16.7 %all-to-all-start.5 = ((bf16[128,1,4,128]{3,2,1,0:T(4,128)(2,1)}), bf16[128,1,4,128]{3,2,1,0:T(4,128)(2,1)}, u32[]{:S(2)}, u32[]{:S(2)}) async-start(bf16[128,1,4,128]{3,2,1,0:T(4,128)(2,1)} %copy.176), calls=%async_computation.5 | async-start | bytes 262144 | tf_op jit(solution)/shard_map/all_to_all | solution.py:428
  157.2 18.4 %all-to-all-start.6 = ((bf16[128,1,4,128]{3,2,1,0:T(4,128)(2,1)}), bf16[128,1,4,128]{3,2,1,0:T(4,128)(2,1)}, u32[]{:S(2)}, u32[]{:S(2)}) async-start(bf16[128,1,4,128]{3,2,1,0:T(4,128)(2,1)} %copy.184), calls=%async_computation.6 | async-start | bytes 262144 | tf_op jit(solution)/shard_map/all_to_all | solution.py:429
  175.6 21.9 %all-to-all-start.7 = ((bf16[128,1,4,128]{3,2,1,0:T(4,128)(2,1)}), bf16[128,1,4,128]{3,2,1,0:T(4,128)(2,1)}, u32[]{:S(2)}, u32[]{:S(2)}) async-start(bf16[128,1,4,128]{3,2,1,0:T(4,128)(2,1)} %copy.192), calls=%async_computation.7 | async-start | bytes 262144 | tf_op jit(solution)/shard_map/all_to_all | solution.py:430
  206.4 53.8 %copy-start.49 = (f32[128]{0:T(128)S(1)}, f32[128]{0:T(128)}, u32[]{:S(2)}) copy-start(f32[128]{0:T(128)} %get-tuple-element.22) | copy-start | bytes 1540
  206.4 53.8 %copy-start.6 = (f32[128,512]{1,0:T(8,128)S(1)}, f32[128,512]{1,0:T(8,128)}, u32[]{:S(2)}) copy-start(f32[128,512]{1,0:T(8,128)} %copy-done.5) | copy-start | bytes 786436
  206.4 53.8 %copy-start.38 = (f32[512]{0:T(512)S(1)}, f32[512]{0:T(512)}, u32[]{:S(2)}) copy-start(f32[512]{0:T(512)} %param.15) | copy-start | bytes 6148
  206.4 53.8 %copy-start.40 = (f32[512]{0:T(512)S(1)}, f32[512]{0:T(512)}, u32[]{:S(2)}) copy-start(f32[512]{0:T(512)} %param.14) | copy-start | bytes 6148
  206.4 53.8 %copy-start.42 = (f32[128]{0:T(128)S(1)}, f32[128]{0:T(128)}, u32[]{:S(2)}) copy-start(f32[128]{0:T(128)} %copy-done.41) | copy-start | bytes 1540
  206.4 53.8 %copy-start.45 = (f32[128]{0:T(128)S(1)}, f32[128]{0:T(128)}, u32[]{:S(2)}) copy-start(f32[128]{0:T(128)} %copy-done.43) | copy-start | bytes 1540
  206.4 53.8 %copy-start.47 = (f32[128]{0:T(128)S(1)}, f32[128]{0:T(128)}, u32[]{:S(2)}) copy-start(f32[128]{0:T(128)} %copy-done.46) | copy-start | bytes 1540
  208.6 51.6 %copy-start.8 = (f32[128,512]{1,0:T(8,128)S(1)}, f32[128,512]{1,0:T(8,128)}, u32[]{:S(2)}) copy-start(f32[128,512]{1,0:T(8,128)} %copy-done.7) | copy-start | bytes 786436
  208.6 51.6 %copy-start.12 = (bf16[1,2,8,8,512]{4,3,2,1,0:T(8,128)(2,1)S(1)}, bf16[1,2,8,8,512]{4,3,2,1,0:T(8,128)(2,1)}, u32[]{:S(2)}) copy-start(bf16[1,2,8,8,512]{4,3,2,1,0:T(8,128)(2,1)} %param.8) | copy-start | bytes 393220
  208.6 51.6 %copy-start.34 = (f32[128,512]{1,0:T(8,128)S(1)}, f32[128,512]{1,0:T(8,128)}, u32[]{:S(2)}) copy-start(f32[128,512]{1,0:T(8,128)} %get-tuple-element.41) | copy-start | bytes 786436
  (34 other events, 118.1 us)

commit v2 on v0

v2 whole, which is shorter than its diff:
```python
import functools
import math
import types

import jax
import jax.numpy as jnp
from jax import lax
from jax.experimental import pallas as pl
from jax.experimental.pallas import tpu as pltpu
from jax.sharding import PartitionSpec as P

MESH = pl.DeviceIdType.MESH
F32 = jnp.float32
BF16 = jnp.bfloat16
EPSILON = 1e-06
ROOT = math.sqrt(2.0 / math.pi)
LOWEST = -1e30
SLABS = 64


def places():
    slab, case = lax.axis_index("slab"), lax.axis_index("case")
    return slab // 16, (slab // 2) % 8, slab % 2, case // 2, case % 2


def device(x, z, y_hi, y_lo, core):
    return ((x * 8 + z) * 2 + y_hi, y_lo * 2 + core)


def remote(src, dst, send_sem, recv_sem, to):
    copy = pltpu.make_async_remote_copy(
        src_ref=src, dst_ref=dst, send_sem=send_sem, recv_sem=recv_sem, device_id=to, device_id_type=MESH
    )
    copy.start()
    return copy


def nn(a, b):
    return lax.dot_general(a, b, (((1,), (0,)), ((), ())), preferred_element_type=F32)


def nt(a, b):
    return lax.dot_general(a, b, (((1,), (1,)), ((), ())), preferred_element_type=F32)


def tn(a, b):
    return lax.dot_general(a, b, (((0,), (0,)), ((), ())), preferred_element_type=F32)


def to_rows(grid):
    first, second = grid[0], grid[1]
    low = lax.broadcasted_iota(jnp.int32, first.shape, 1) < 4
    even = jnp.where(low, first, pltpu.roll(second, 4, 1))
    odd = jnp.where(low, pltpu.roll(first, 4, 1), second)
    return jnp.stack([even, odd], axis=1).reshape(128, first.shape[-1])


def to_grid(rows):
    split = rows.reshape(8, 2, 8, rows.shape[-1])
    even, odd = split[:, 0], split[:, 1]
    low = lax.broadcasted_iota(jnp.int32, even.shape, 1) < 4
    first = jnp.where(low, even, pltpu.roll(odd, 4, 1))
    second = jnp.where(low, pltpu.roll(even, 4, 1), odd)
    return first, second


def norm_stats(values):
    inverse = lax.rsqrt(jnp.mean(values * values, axis=-1, keepdims=True) + EPSILON)
    return values * inverse, inverse


def norm_back(grad_normed, normed, inverse, gain):
    scaled = grad_normed * gain
    return inverse * (scaled - normed * jnp.mean(scaled * normed, axis=-1, keepdims=True))


def two_heads(pair):
    lane = lax.broadcasted_iota(jnp.int32, (128, 128), 1)
    first = jnp.where(lane < 64, 1.0, 0.0).astype(BF16)
    second = jnp.where(lane < 64, 0.0, 1.0).astype(BF16)
    return jnp.concatenate([pair * first, pair * second], axis=0)


def over_keys(across):
    return jnp.concatenate([across[:, 0:128], across[:, 128:256]], axis=0)


def line_probs(scores, mask):
    if mask is not None:
        scores = jnp.where(mask, scores, LOWEST)
    weights = jnp.exp(scores - jnp.max(scores, axis=0, keepdims=True))
    return weights * (1.0 / jnp.sum(weights, axis=0, keepdims=True))


def line_masks():
    keys = lax.broadcasted_iota(jnp.int32, (128, 256), 0)
    queries = lax.broadcasted_iota(jnp.int32, (128, 256), 1) & 127
    apart = keys ^ queries
    return (apart & 0x74) == 0, (apart & 0x0F) == 0


def pair_scores(queries, keys):
    return nt(keys, two_heads(queries * jnp.array(0.125, BF16)))


def pair_out(probs, values):
    return tn(over_keys(probs), two_heads(values))


def score_grads(probs, grad_probs):
    return probs * (grad_probs - jnp.sum(probs * grad_probs, axis=0, keepdims=True))


def pair_back(rounded, grad_scores, queries, keys, grads):
    both = two_heads(grads)
    grad_values = nn(rounded, both)
    grad_keys = nn(grad_scores, two_heads(queries * jnp.array(0.125, BF16)))
    grad_queries = tn(over_keys(grad_scores), two_heads(keys)) * 0.125
    return grad_queries, grad_keys, grad_values


class Ring:
    def __init__(self, me, dev, part, relay, fin, ss, rs):
        self.me, self.dev, self.part, self.relay, self.fin, self.ss, self.rs = me, dev, part, relay, fin, ss, rs
        self.right, self.left, self.over = (me + 1) % 4, (me + 3) % 4, (me + 2) % 4
        self.copies = []

    def send(self, src, dst, to):
        n = len(self.copies)
        self.copies.append(remote(src, dst, self.ss.at[n], self.rs.at[n], self.dev(to)))

    def start(self):
        self.send(self.part(self.over, 0), self.relay.at[0], self.right)
        self.send(self.part(self.over, 1), self.relay.at[1], self.left)
        self.send(self.part(self.right, 1), self.fin.at[1], self.right)
        self.send(self.part(self.left, 0), self.fin.at[2], self.left)

    def middle(self):
        for h, to, slot in ((0, self.right, 0), (1, self.left, 3)):
            self.copies[h].wait_recv()
            ref = self.part(to, h)
            ref[...] = (ref[...].astype(F32) + self.relay[h].astype(F32)).astype(BF16)
            self.send(ref, self.fin.at[slot], to)

    def finish(self):
        for copy in self.copies[2:]:
            copy.wait_recv()

    def result(self, h):
        a, b = (0, 2) if h == 0 else (1, 3)
        own = self.part(self.me, h)[...].astype(F32)
        return (own + self.fin[a].astype(F32) + self.fin[b].astype(F32)).astype(BF16)

    def drain(self):
        for copy in self.copies:
            copy.wait_send()


def sum_shapes(wide):
    vm, dma, part = pltpu.VMEM, pltpu.SemaphoreType.DMA, wide // 2
    return dict(
        buf=vm((4, 8, 2, 16, wide), BF16),
        relay_a=vm((2, 2, 2, 16, wide), BF16), fin_a=vm((4, 2, 2, 16, wide), BF16),
        relay_b=vm((2, 2, 4, 16, part), BF16), fin_b=vm((4, 2, 4, 16, part), BF16),
        a1=vm((4, 2, 16, wide), BF16), b1=vm((4, 4, 16, part), BF16),
        relay_a2=vm((2, 2, 16, part), BF16), fin_a2=vm((4, 2, 16, part), BF16),
        relay_b2=vm((2, 2, 16, part), BF16), fin_b2=vm((4, 2, 16, part), BF16),
        zbuf=vm((8, 16, part), BF16), zrecv=vm((7, 16, part), BF16), gath=vm((4, 16, part), BF16),
        ss_ring=dma((4, 6)), rs_ring=dma((4, 6)), ss_z=dma((7,)), rs_z=dma((7,)), ss_g=dma((3,)), rs_g=dma((3,)),
    )


class Sum:
    def __init__(self, ref):
        self.ref = ref
        x, z, y_hi, y_lo, core = places()
        self.place = (x, z, y_hi, y_lo, core)
        y = y_hi * 2 + y_lo
        part = ref.zbuf.shape[-1]

        def lanes(lo):
            return pl.ds(pl.multiple_of(lo * part, 128), part)

        def dev_x(i):
            return device(i, z, y_hi, y_lo, core)

        def dev_y(i):
            return device(x, z, i // 2, i % 2, core)

        sems = [(ref.ss_ring.at[i], ref.rs_ring.at[i]) for i in range(4)]
        self.a = Ring(x, dev_x, lambda i, h: ref.buf.at[i, pl.ds(2 * h, 2)], ref.relay_a, ref.fin_a, *sems[0])
        self.b = Ring(
            y, dev_y, lambda i, h: ref.buf.at[pl.ds(2 * h, 2), pl.ds(4, 4), i // 2, :, lanes(i % 2)],
            ref.relay_b, ref.fin_b, *sems[1],
        )
        self.a2 = Ring(
            y, dev_y, lambda i, h: ref.a1.at[pl.ds(2 * h, 2), i // 2, :, lanes(i % 2)],
            ref.relay_a2, ref.fin_a2, *sems[2],
        )
        self.b2 = Ring(x, dev_x, lambda i, h: ref.b1.at[i, pl.ds(2 * h, 2)], ref.relay_b2, ref.fin_b2, *sems[3])
        self.copies = []

    def put(self, at, upper, lower):
        width = upper.shape[-1]
        both = jnp.concatenate([upper, lower], axis=1).astype(BF16)
        self.ref.buf[:, :, :, :, at : at + width] = both.reshape(4, 8, 2, 16, width)

    def start(self):
        self.a.start()
        self.b.start()

    def middle(self):
        self.a.middle()
        self.b.middle()

    def second(self):
        self.a.finish()
        for h in range(2):
            self.ref.a1[2 * h : 2 * h + 2] = self.a.result(h)
        self.a2.start()
        self.b.finish()
        for h in range(2):
            self.ref.b1[2 * h : 2 * h + 2] = self.b.result(h)
        self.b2.start()

    def second_middle(self):
        self.a2.middle()
        self.b2.middle()

    def along_z(self):
        ref = self.ref
        x, z, y_hi, y_lo, core = self.place
        self.a2.finish()
        for h in range(2):
            ref.zbuf[2 * h : 2 * h + 2] = self.a2.result(h)
        self.b2.finish()
        for h in range(2):
            ref.zbuf[4 + 2 * h : 6 + 2 * h] = self.b2.result(h)
        for d in range(1, 8):
            to = (z + d) % 8
            self.copies.append(
                remote(ref.zbuf.at[to], ref.zrecv.at[d - 1], ref.ss_z.at[d - 1], ref.rs_z.at[d - 1],
                       device(x, to, y_hi, y_lo, core))
            )

    def gather(self):
        ref = self.ref
        x, z, y_hi, y_lo, core = self.place
        total = ref.zbuf[z].astype(F32)
        for d in range(7):
            self.copies[d].wait_recv()
            total = total + ref.zrecv[d].astype(F32)
        mine = y_lo * 2 + core
        ref.gath[mine] = total.astype(BF16)
        for n, (dy, dc) in enumerate(((0, 1), (1, 0), (1, 1))):
            to = device(x, z, y_hi, (y_lo + dy) % 2, (core + dc) % 2)
            self.copies.append(remote(ref.gath.at[mine], ref.gath.at[mine], ref.ss_g.at[n], ref.rs_g.at[n], to))

    def finish(self):
        for copy in self.copies[7:]:
            copy.wait_recv()
        gath = self.ref.gath
        return [jnp.concatenate([gath[c].astype(F32), gath[2 + c].astype(F32)], axis=1) for c in range(2)]

    def drain(self):
        for copy in self.copies:
            copy.wait_send()
        for ring in (self.a, self.b, self.a2, self.b2):
            ring.drain()


class Exchange:
    def __init__(self, send, recv, ss, rs):
        self.send, self.recv, self.ss, self.rs = send, recv, ss, rs

    def start(self):
        me, case = lax.axis_index("slab"), lax.axis_index("case")

        def one(d, carry):
            to = (me + d) % SLABS
            remote(self.send.at[to], self.recv.at[me], self.ss, self.rs, (to, case))
            return carry

        lax.fori_loop(1, SLABS, one, 0)
        self.recv[me] = self.send[me]

    def wait(self):
        got = self.recv.at[pl.ds(0, SLABS - 1)]
        pltpu.make_async_copy(got, got, self.rs).wait()

    def drain(self):
        sent = self.send.at[pl.ds(0, SLABS - 1)]
        pltpu.make_async_copy(sent, sent, self.ss).wait()


def by_pair(blocks):
    width = blocks[0].shape[-1]
    return jnp.stack([b.reshape(16, 8, width) for b in blocks], axis=1).reshape(SLABS, 8, width)


def scratch():
    vm, dma = pltpu.VMEM, pltpu.SemaphoreType.DMA
    return dict(
        wq=vm((512, 1536), BF16), wo=vm((512, 512), BF16), wu=vm((512, 2048), BF16), wd=vm((2048, 512), BF16),
        sw=dma((4,)),
        qkv=vm((128, 1536), BF16),
        qsend=vm((SLABS, 8, 384), BF16), qrecv=vm((SLABS, 8, 384), BF16),
        osend=vm((SLABS, 8, 128), BF16), orecv=vm((SLABS, 8, 128), BF16),
        gsend=vm((SLABS, 8, 128), BF16), grecv=vm((SLABS, 8, 128), BF16),
        dsend=vm((SLABS, 8, 384), BF16), drecv=vm((SLABS, 8, 384), BF16),
        ss_x=dma((4,)), rs_x=dma((4,)),
        z32=vm((3, 512, 128), F32), o32=vm((512, 128), F32), g32=vm((512, 128), F32), d32=vm((3, 512, 128), F32),
        px=vm((4, 128, 256), F32), py=vm((4, 128, 256), F32), pz=vm((4, 128, 256), F32),
        oxy=vm((128, 512), F32), dxy=vm((128, 1536), F32), gmix=vm((128, 512), BF16),
        gact=vm((128, 2048), F32), flat=vm((128, 512), F32), gres=vm((128, 512), F32),
        b_h1=vm((256, 512), BF16), b_mixed=vm((256, 512), BF16), b_h2=vm((256, 512), BF16), b_act=vm((256, 2048), BF16),
        cot=vm((128, 512), BF16), gu=vm((128, 2048), BF16), grb=vm((128, 512), BF16), gp=vm((128, 1536), BF16),
        b_cot=vm((256, 256), BF16), b_gu=vm((256, 1024), BF16), b_grb=vm((256, 256), BF16), b_gp=vm((256, 768), BF16),
        ss_core=dma((8,)), rs_core=dma((8,)),
        down32=vm((SLABS, 32, 256), F32), gain32=vm((SLABS, 8, 128), F32),
        one=sum_shapes(1280), two=sum_shapes(512),
    )


def kernel(factor, tree, tok, cot, wq_h, wo_h, wu_h, wd_h, ga, gm, o_tok, o_qkv, o_out, o_up, o_down, o_g1, o_g2, *refs):
    r = jax.tree.unflatten(tree, refs)
    r, r_one, r_two = types.SimpleNamespace(**r), types.SimpleNamespace(**r["one"]), types.SimpleNamespace(**r["two"])
    x, z, y_hi, y_lo, core = places()
    slab, case = lax.axis_index("slab"), lax.axis_index("case")
    other = device(x, z, y_hi, y_lo, 1 - core)

    loads = [
        pltpu.make_async_copy(src, dst, r.sw.at[n])
        for n, (src, dst) in enumerate(((wq_h, r.wq), (wo_h, r.wo), (wd_h, r.wd), (wu_h, r.wu)))
    ]
    for load in loads:
        load.start()

    barrier = pltpu.get_barrier_semaphore()

    def greet(d, carry):
        pl.semaphore_signal(barrier, inc=1, device_id=((slab + d) % SLABS, case), device_id_type=MESH)
        return carry

    lax.fori_loop(1, SLABS, greet, 0)
    for peer in (
        other,
        device(x, z, y_hi, 1 - y_lo, core),
        device(x, z, y_hi, 1 - y_lo, 1 - core),
        device(x, z, 1 - y_hi, 1 - y_lo, core),
    ):
        pl.semaphore_signal(barrier, inc=1, device_id=peer, device_id_type=MESH)

    gain_one, gain_two = ga[...], gm[...]
    r.flat[...] = to_rows(tok[...].astype(F32))
    normed_one, inverse_one = norm_stats(r.flat[...])
    r.b_h1[0:128, :] = (normed_one * gain_one).astype(BF16)
    r.cot[...] = to_rows(cot[...].astype(F32)).astype(BF16)
    loads[0].wait()
    for i in range(3):
        r.qkv[:, 512 * i : 512 * i + 512] = nn(r.b_h1[0:128, :], r.wq[:, 512 * i : 512 * i + 512]).astype(BF16)
    for i in range(3):
        r.qsend[:, :, 128 * i : 128 * i + 128] = by_pair(
            [r.qkv[:, 512 * i + 128 * j : 512 * i + 128 * j + 128].astype(F32) for j in range(4)]
        ).astype(BF16)
    pl.semaphore_wait(barrier, SLABS + 3)
    ex_q = Exchange(r.qsend, r.qrecv, r.ss_x.at[0], r.rs_x.at[0])
    ex_o = Exchange(r.osend, r.orecv, r.ss_x.at[1], r.rs_x.at[1])
    ex_g = Exchange(r.gsend, r.grecv, r.ss_x.at[2], r.rs_x.at[2])
    ex_d = Exchange(r.dsend, r.drecv, r.ss_x.at[3], r.rs_x.at[3])
    ex_q.start()

    core_copies = []

    def to_core_full(ref):
        n = len(core_copies)
        core_copies.append(
            remote(ref.at[pl.ds(0, 128)], ref.at[pl.ds(128, 128)], r.ss_core.at[n], r.rs_core.at[n], other)
        )

    def to_core_half(src, dst):
        n, half = len(core_copies), dst.shape[-1]
        theirs = src.at[:, pl.ds(pl.multiple_of((1 - core) * half, 128), half)]
        core_copies.append(remote(theirs, dst.at[pl.ds(128, 128)], r.ss_core.at[n], r.rs_core.at[n], other))
        dst[0:128, :] = src[:, pl.ds(pl.multiple_of(core * half, 128), half)]

    to_core_full(r.b_h1)
    to_core_half(r.cot, r.b_cot)

    def pair(j):
        return [r.qkv[:, 512 * i + 128 * j : 512 * i + 128 * j + 128] for i in range(3)]

    mask_x, mask_y = line_masks()
    for j in range(4):
        queries, keys, values = pair(j)
        scores = pair_scores(queries, keys)
        r.px[j] = line_probs(scores, mask_x)
        r.py[j] = line_probs(scores, mask_y)
        r.oxy[:, 128 * j : 128 * j + 128] = pair_out((r.px[j] + r.py[j]).astype(BF16), values)

    ex_q.wait()
    for i in range(3):
        r.z32[i] = r.qrecv[:, :, 128 * i : 128 * i + 128].astype(F32).reshape(512, 128)

    def line(j):
        return [r.z32[i, pl.ds(j, 128, stride=4), :].astype(BF16) for i in range(3)]

    for j in range(4):
        queries, keys, values = line(j)
        probs = line_probs(pair_scores(queries, keys), None)
        r.pz[j] = probs
        r.o32[pl.ds(j, 128, stride=4), :] = pair_out(probs.astype(BF16), values)
    r.osend[...] = r.o32[...].reshape(SLABS, 8, 128).astype(BF16)
    ex_o.start()
    loads[2].wait()
    for i in range(4):
        at = slice(512 * i, 512 * i + 512)
        r.gact[:, at] = nt(r.cot[...], r.wd[at, :])

    loads[1].wait()
    loads[3].wait()
    ex_o.wait()
    from_z = r.orecv[...].astype(F32).reshape(16, 4, 8, 128)
    for j in range(4):
        at = slice(128 * j, 128 * j + 128)
        r.b_mixed[0:128, at] = (r.oxy[:, at] + from_z[:, j].reshape(128, 128)).astype(BF16)
    residual = (r.flat[...] + nn(r.b_mixed[0:128, :], r.wo[...])).astype(BF16)
    normed_two, inverse_two = norm_stats(residual.astype(F32))
    r.b_h2[0:128, :] = (normed_two * gain_two).astype(BF16)
    grad_hidden_two = jnp.zeros((128, 512), F32)
    for i in range(4):
        at = slice(512 * i, 512 * i + 512)
        u = nn(r.b_h2[0:128, :], r.wu[:, at])
        square = u * u
        tangent = jnp.tanh(ROOT * u * (1.0 + 0.044715 * square))
        half = 0.5 * (1.0 + tangent)
        r.b_act[0:128, at] = (u * half).astype(BF16)
        slope = half + 0.5 * u * (1.0 - tangent * tangent) * ROOT * (1.0 + 3.0 * 0.044715 * square)
        r.gu[:, at] = (r.gact[:, at] * slope).astype(BF16)
        grad_hidden_two = grad_hidden_two + nt(r.gu[:, at], r.wu[:, at])
    r.gres[...] = r.cot[...].astype(F32) + norm_back(grad_hidden_two, normed_two, inverse_two, gain_two)
    r.grb[...] = r.gres[...].astype(BF16)
    r.gmix[...] = nt(r.grb[...], r.wo[...]).astype(BF16)
    r.gsend[...] = by_pair([r.gmix[:, 128 * j : 128 * j + 128].astype(F32) for j in range(4)]).astype(BF16)
    ex_g.start()
    to_core_full(r.b_act)
    to_core_half(r.gu, r.b_gu)
    to_core_full(r.b_h2)
    to_core_full(r.b_mixed)
    to_core_half(r.grb, r.b_grb)
    ones = jnp.ones((128, 128), BF16)
    r.gain32[...] = tn((grad_hidden_two * normed_two).astype(BF16), ones).reshape(SLABS, 8, 128)

    one, two = Sum(r_one), Sum(r_two)
    for copy in core_copies:
        copy.wait_recv()
    r.down32[...] = tn(r.b_act[...], r.b_cot[...]).reshape(SLABS, 32, 256)
    for i in range(2):
        one.put(
            256 * i,
            tn(r.b_h2[...], r.b_gu[:, 256 * i : 256 * i + 256]).reshape(SLABS, 8, 256),
            tn(r.b_h2[...], r.b_gu[:, 512 + 256 * i : 768 + 256 * i]).reshape(SLABS, 8, 256),
        )
    one.put(512, r.down32[:, 0:8, :], r.down32[:, 16:24, :])
    one.put(768, r.down32[:, 8:16, :], r.down32[:, 24:32, :])
    upper = tn(r.b_mixed[...], r.b_grb[...]).reshape(SLABS, 8, 256)
    one.put(1024, upper[:, :, 0:128], r.gain32[...])
    one.put(1152, upper[:, :, 128:256], jnp.zeros((SLABS, 8, 128), F32))
    one.start()

    ex_g.wait()
    r.g32[...] = r.grecv[...].astype(F32).reshape(512, 128)
    for j in range(4):
        queries, keys, values = line(j)
        grads = r.g32[pl.ds(j, 128, stride=4), :].astype(BF16)
        probs = r.pz[j]
        grad_scores = score_grads(probs, nt(values, two_heads(grads))).astype(BF16)
        back = pair_back(probs.astype(BF16), grad_scores, queries, keys, grads)
        for i in range(3):
            r.d32[i, pl.ds(j, 128, stride=4), :] = back[i]
    for i in range(3):
        r.dsend[:, :, 128 * i : 128 * i + 128] = r.d32[i].reshape(SLABS, 8, 128).astype(BF16)
    ex_d.start()

    for j in range(4):
        queries, keys, values = pair(j)
        grads = r.gmix[:, 128 * j : 128 * j + 128]
        grad_probs = nt(values, two_heads(grads))
        probs_x, probs_y = r.px[j], r.py[j]
        grad_scores = (score_grads(probs_x, grad_probs) + score_grads(probs_y, grad_probs)).astype(BF16)
        back = pair_back((probs_x + probs_y).astype(BF16), grad_scores, queries, keys, grads)
        for i in range(3):
            r.dxy[:, 512 * i + 128 * j : 512 * i + 128 * j + 128] = back[i]

    one.middle()

    ex_d.wait()
    for i in range(3):
        from_z = r.drecv[:, :, 128 * i : 128 * i + 128].astype(F32).reshape(16, 4, 8, 128)
        for j in range(4):
            at = slice(512 * i + 128 * j, 512 * i + 128 * j + 128)
            r.gp[:, at] = (r.dxy[:, at] + from_z[:, j].reshape(128, 128)).astype(BF16)
    to_core_half(r.gp, r.b_gp)
    grad_hidden_one = nt(r.gp[...], r.wq[...])
    normed_one, inverse_one = norm_stats(r.flat[...])
    first, second = to_grid(r.gres[...] + norm_back(grad_hidden_one, normed_one, inverse_one, gain_one))
    o_tok[0] = first.astype(BF16)
    o_tok[1] = second.astype(BF16)
    gains = tn((grad_hidden_one * normed_one).astype(BF16), ones).reshape(SLABS, 8, 128)
    one.second()
    core_copies[-1].wait_recv()
    parts = [tn(r.b_h1[...], r.b_gp[:, 256 * i : 256 * i + 256]).reshape(SLABS, 8, 256) for i in range(3)]
    two.put(0, parts[0], parts[2])
    two.put(256, parts[1][:, :, 0:128], gains)
    two.put(384, parts[1][:, :, 128:256], jnp.zeros((SLABS, 8, 128), F32))
    two.start()
    one.second_middle()
    two.middle()
    one.along_z()
    two.second()
    one.gather()
    two.second_middle()
    two.along_z()
    gain = jnp.zeros((8, 128), F32)
    for c, full in enumerate(one.finish()):
        full = full * factor
        o_up[:, 1024 * c : 1024 * c + 512] = full[0:8, 0:512]
        o_up[:, 1024 * c + 512 : 1024 * c + 1024] = full[8:16, 0:512]
        at = slice(256 * c, 256 * c + 256)
        o_down[0:8, at] = full[0:8, 512:768]
        o_down[8:16, at] = full[0:8, 768:1024]
        o_down[16:24, at] = full[8:16, 512:768]
        o_down[24:32, at] = full[8:16, 768:1024]
        o_out[:, at] = full[0:8, 1024:1280]
        gain = gain + full[8:16, 1024:1152]
    o_g2[...] = gain
    two.gather()
    gain = jnp.zeros((8, 128), F32)
    for c, full in enumerate(two.finish()):
        full = full * factor
        o_qkv[:, 768 * c : 768 * c + 512] = full[0:8, 0:512]
        o_qkv[:, 768 * c + 512 : 768 * c + 768] = full[8:16, 0:256]
        gain = gain + full[8:16, 256:384]
    o_g1[...] = gain

    for exchange in (ex_q, ex_o, ex_g, ex_d):
        exchange.drain()
    for copy in core_copies:
        copy.wait_send()
    one.drain()
    two.drain()


def body(tokens, cotangent, w_qkv, w_out, w_up, w_down, gain_attn, gain_mlp):
    width = tokens.shape[-1]
    factor = 1.0 / math.sqrt(128 * lax.axis_size("slab") * lax.axis_size("case"))
    shapes = scratch()
    leaves, tree = jax.tree.flatten(shapes)
    vmem, any_space = pl.BlockSpec(memory_space=pltpu.VMEM), pl.BlockSpec(memory_space=pl.ANY)
    outs = ((8, 1536), (8, 512), (8, 2048), (32, 512), (8, 128), (8, 128))
    result = pl.pallas_call(
        functools.partial(kernel, factor, tree),
        out_shape=[jax.ShapeDtypeStruct((2, 8, 8, width), BF16)] + [jax.ShapeDtypeStruct(s, F32) for s in outs],
        in_specs=[vmem, vmem] + [any_space] * 4 + [vmem, vmem],
        out_specs=[vmem] * 7,
        scratch_shapes=leaves,
        compiler_params=pltpu.CompilerParams(
            collective_id=1, has_side_effects=True, vmem_limit_bytes=56 * 1024 * 1024
        ),
        cost_estimate=pl.CostEstimate(flops=3_500_000_000, bytes_accessed=7_000_000, transcendentals=0),
    )(
        tokens.reshape(2, 8, 8, width),
        cotangent.reshape(2, 8, 8, width),
        w_qkv,
        w_out,
        w_up,
        w_down,
        gain_attn.reshape(1, width),
        gain_mlp.reshape(1, width),
    )
    return (
        result[0].reshape(tokens.shape),
        result[1],
        result[2],
        result[3],
        result[4],
        result[5][:, 0],
        result[6][:, 0],
    )


def solution(mesh):
    grid = P("case", "slab", None, None, None)
    return jax.shard_map(
        body,
        mesh=mesh,
        in_specs=(grid, grid, P(), P(), P(), P(), P(), P()),
        out_specs=(grid, P("slab", None), P("slab", None), P("slab", None), P("slab", None), P("slab"), P("slab")),
        check_vma=False,
    )
```

time: 2090 us -> 96.7 us (0.05)
  waiting for transfers between devices: 1720 us -> 0 us
  blocking collectives: 155 us -> 0 us
  Pallas kernels: 0 us -> 87.1 us
  starting transfers between devices: 66.9 us -> 0 us
  matrix products: 53.8 us -> 0 us
  local copies, waits for them, and re-layouts: 50.5 us -> 8.63 us
  other arithmetic: 25.2 us -> 0 us
    reduce_scatter x4 -> x0, waiting for transfers between devices: 1580 us -> none  [the longest x1 831 us: body(): lax.psum_scatter(total_qkv, 'slab', scatter_dimension=0, tiled=True)]
    unnamed x1 -> x0, blocking collectives: 155 us -> none
    psum x1 -> x0, waiting for transfers between devices: 87.4 us -> none  [body(): lax.psum(shares[0].astype(jnp.bfloat16), 'case').astype(jnp.float32)]
    pallas_call x0 -> x1, Pallas kernels: none -> 87.1 us  [body(): pl.pallas_call(functools.partial(kernel, factor, tree), out_shape=[jax.Sh...]
    all_to_all x8 -> x0, starting transfers between devices: 66.7 us -> none  [the longest x1 15.1 us: body(): lax.all_to_all(value_block, 'slab', split_axis=1, concat_axis=0, tiled=True)]
    dot_general x28 -> x0, matrix products: 48.8 us -> none  [the longest x3 7.12 us: attend_back(): jnp.einsum('bhlm,blhe->bmhe', rounded, grad_lines, preferred_element_type...]
    all_to_all x8 -> x0, waiting for transfers between devices: 44.7 us -> none  [the longest x1 10.3 us: body(): lax.all_to_all(value_block, 'slab', split_axis=1, concat_axis=0, tiled=True)]
  transfers between devices with their start and end apart: 13 -> 0, of which waited for: 13 -> 0; matrix products, arithmetic and copies ran while one was open for 4% -> 0% of each run, Pallas kernels for 0% -> 0%
where the time goes in v2:
time: 96.7 us; the launch traced here: 96.4 us
  Pallas kernels  87.1 us (90%)
  local copies, waits for them, and re-layouts  8.63 us (9%)
    pallas_call x1, Pallas kernels, body(): pl.pallas_call(functools.partial(kernel, factor, tree), out_shape=[jax.Sh...  87.1 us
    unnamed x5, local copies, waits for them, and re-layouts  7.25 us

profile of v2, /device:TPU:1, one launch (start us, length us, event | category | flops | bytes accessed | tf_op | source)
XLA Modules:
  0.0 96.4 jit_solution(190703351132536113)
XLA Ops:
  0.6 87.1 %shard_map.135 = (bf16[2,8,8,512]{3,2,1,0:T(8,128)(2,1)}, f32[8,1536]{1,0:T(8,128)}, f32[8,512]{1,0:T(8,128)}, f32[8,2048]{1,0:T(8,128)}, f32[32,512]{1,0:T(8,128)}, /*index=5*/f32[8,128]{1,0:T(8,128)}, f32[8,128]{1,0:T(8,128)}) custom-call(bf16[2,8,8,512]{3,2,1,0:T(8,128)(2,1)} %bitcast.6, bf16[2,8,8,512]{3,2,1,0:T(8,128)(2,1)} %bitcast.7, ...), custom_call_target="tpu_custom_call" | custom-call | flops 3500000000 | bytes 7000000 | tf_op jit(solution)/shard_map/pallas_call | solution.py:561
  87.8 1.4 %slice_reduce_fusion = (f32[8]{0:T(128)}, f32[8]{0:T(128)}) fusion(f32[8,128]{1,0:T(8,128)} %get-tuple-element.20, f32[8,128]{1,0:T(8,128)} %get-tuple-element.19), kind=kLoop, calls=%fused_computation | loop fusion | bytes 128 | tf_op jit(solution)/shard_map/slice | solution.py:588
  89.1 1.6 %copy.20 = bf16[1,2,8,8,512]{4,3,2,1,0:T(8,128)(2,1)} copy(bf16[1,2,8,8,512]{4,3,2,1,0:T(8,128)(2,1)} %bitcast.5) | data formatting | bytes 262144
  90.7 1.4 %copy.21 = f32[8,1536]{1,0:T(8,128)} copy(f32[8,1536]{1,0:T(8,128)} %get-tuple-element.31) | data formatting | bytes 98304
  92.1 1.3 %copy.22 = f32[8,512]{1,0:T(8,128)} copy(f32[8,512]{1,0:T(8,128)} %get-tuple-element.32) | data formatting | bytes 32768
  93.4 1.5 %copy.23 = f32[8,2048]{1,0:T(8,128)} copy(f32[8,2048]{1,0:T(8,128)} %get-tuple-element.33) | data formatting | bytes 131072
  94.9 1.5 %copy.24 = f32[32,512]{1,0:T(8,128)} copy(f32[32,512]{1,0:T(8,128)} %get-tuple-element.34) | data formatting | bytes 131072

commit v3 on v2

--- a/solution.py
+++ b/solution.py
@@ -130,44 +130,51 @@
         self.copies.append(remote(src, dst, self.ss.at[n], self.rs.at[n], self.dev(to)))
 
     def start(self):
+        if self.relay is None:
+            for n, to in enumerate((self.over, self.right, self.left)):
+                for h in range(2):
+                    self.send(self.part(to, h), self.fin.at[n, h], to)
+            return
         self.send(self.part(self.over, 0), self.relay.at[0], self.right)
         self.send(self.part(self.over, 1), self.relay.at[1], self.left)
-        self.send(self.part(self.right, 1), self.fin.at[1], self.right)
-        self.send(self.part(self.left, 0), self.fin.at[2], self.left)
+        self.send(self.part(self.right, 1), self.fin.at[0, 1], self.right)
+        self.send(self.part(self.left, 0), self.fin.at[0, 0], self.left)
 
     def middle(self):
-        for h, to, slot in ((0, self.right, 0), (1, self.left, 3)):
+        for h, to in ((0, self.right), (1, self.left)):
             self.copies[h].wait_recv()
             ref = self.part(to, h)
             ref[...] = (ref[...].astype(F32) + self.relay[h].astype(F32)).astype(BF16)
-            self.send(ref, self.fin.at[slot], to)
+            self.send(ref, self.fin.at[1, h], to)
 
     def finish(self):
-        for copy in self.copies[2:]:
+        for copy in self.copies[0 if self.relay is None else 2 :]:
             copy.wait_recv()
 
     def result(self, h):
-        a, b = (0, 2) if h == 0 else (1, 3)
-        own = self.part(self.me, h)[...].astype(F32)
-        return (own + self.fin[a].astype(F32) + self.fin[b].astype(F32)).astype(BF16)
+        total = self.part(self.me, h)[...].astype(F32)
+        for n in range(3 if self.relay is None else 2):
+            total = total + self.fin[n, h].astype(F32)
+        return total.astype(BF16)
 
     def drain(self):
         for copy in self.copies:
             copy.wait_send()
 
 
-def sum_shapes(wide):
+def sum_shapes(wide, relays):
     vm, dma, part = pltpu.VMEM, pltpu.SemaphoreType.DMA, wide // 2
-    return dict(
+    shapes = dict(
         buf=vm((4, 8, 2, 16, wide), BF16),
-        relay_a=vm((2, 2, 2, 16, wide), BF16), fin_a=vm((4, 2, 2, 16, wide), BF16),
-        relay_b=vm((2, 2, 4, 16, part), BF16), fin_b=vm((4, 2, 4, 16, part), BF16),
+        fin_a=vm((3, 2, 2, 2, 16, wide), BF16), fin_b=vm((3, 2, 2, 4, 16, part), BF16),
         a1=vm((4, 2, 16, wide), BF16), b1=vm((4, 4, 16, part), BF16),
-        relay_a2=vm((2, 2, 16, part), BF16), fin_a2=vm((4, 2, 16, part), BF16),
-        relay_b2=vm((2, 2, 16, part), BF16), fin_b2=vm((4, 2, 16, part), BF16),
+        fin_a2=vm((3, 2, 2, 16, part), BF16), fin_b2=vm((3, 2, 2, 16, part), BF16),
         zbuf=vm((8, 16, part), BF16), zrecv=vm((7, 16, part), BF16), gath=vm((4, 16, part), BF16),
         ss_ring=dma((4, 6)), rs_ring=dma((4, 6)), ss_z=dma((7,)), rs_z=dma((7,)), ss_g=dma((3,)), rs_g=dma((3,)),
     )
+    if relays:
+        shapes.update(relay_a=vm((2, 2, 2, 16, wide), BF16), relay_b=vm((2, 2, 4, 16, part), BF16))
+    return shapes
 
 
 class Sum:
@@ -188,16 +195,17 @@
             return device(x, z, i // 2, i % 2, core)
 
         sems = [(ref.ss_ring.at[i], ref.rs_ring.at[i]) for i in range(4)]
-        self.a = Ring(x, dev_x, lambda i, h: ref.buf.at[i, pl.ds(2 * h, 2)], ref.relay_a, ref.fin_a, *sems[0])
+        relay_a, relay_b = getattr(ref, "relay_a", None), getattr(ref, "relay_b", None)
+        self.a = Ring(x, dev_x, lambda i, h: ref.buf.at[i, pl.ds(2 * h, 2)], relay_a, ref.fin_a, *sems[0])
         self.b = Ring(
             y, dev_y, lambda i, h: ref.buf.at[pl.ds(2 * h, 2), pl.ds(4, 4), i // 2, :, lanes(i % 2)],
-            ref.relay_b, ref.fin_b, *sems[1],
+            relay_b, ref.fin_b, *sems[1],
         )
         self.a2 = Ring(
             y, dev_y, lambda i, h: ref.a1.at[pl.ds(2 * h, 2), i // 2, :, lanes(i % 2)],
-            ref.relay_a2, ref.fin_a2, *sems[2],
+            None, ref.fin_a2, *sems[2],
         )
-        self.b2 = Ring(x, dev_x, lambda i, h: ref.b1.at[i, pl.ds(2 * h, 2)], ref.relay_b2, ref.fin_b2, *sems[3])
+        self.b2 = Ring(x, dev_x, lambda i, h: ref.b1.at[i, pl.ds(2 * h, 2)], None, ref.fin_b2, *sems[3])
         self.copies = []
 
     def put(self, at, upper, lower):
@@ -222,10 +230,6 @@
         for h in range(2):
             self.ref.b1[2 * h : 2 * h + 2] = self.b.result(h)
         self.b2.start()
-
-    def second_middle(self):
-        self.a2.middle()
-        self.b2.middle()
 
     def along_z(self):
         ref = self.ref
@@ -270,26 +274,30 @@
 
 
 class Exchange:
-    def __init__(self, send, recv, ss, rs):
-        self.send, self.recv, self.ss, self.rs = send, recv, ss, rs
+    def __init__(self, send, recv, ss, rs, shared=1):
+        self.send, self.recv, self.ss, self.rs, self.shared = send, recv, ss, rs, shared
 
     def start(self):
-        me, case = lax.axis_index("slab"), lax.axis_index("case")
-
-        def one(d, carry):
-            to = (me + d) % SLABS
-            remote(self.send.at[to], self.recv.at[me], self.ss, self.rs, (to, case))
+        me = lax.axis_index("slab")
+        x, z, y_hi, y_lo, core = places()
+
+        def one(n, carry):
+            kz, kx, ky = n // 8, (n // 2) % 4, n % 2
+            dz = 4 + ((kz + 1) // 2) * (1 - 2 * (kz % 2))
+            dx = 2 + ((kx + 1) // 2) * (1 - 2 * (kx % 2))
+            to = device((x + dx) % 4, (z + dz) % 8, (y_hi + 1 - ky) % 2, y_lo, core)
+            remote(self.send.at[to[0] // self.shared], self.recv.at[me], self.ss, self.rs, to)
             return carry
 
-        lax.fori_loop(1, SLABS, one, 0)
-        self.recv[me] = self.send[me]
+        lax.fori_loop(0, SLABS - 1, one, 0)
+        self.recv[me] = self.send[me // self.shared]
 
     def wait(self):
         got = self.recv.at[pl.ds(0, SLABS - 1)]
         pltpu.make_async_copy(got, got, self.rs).wait()
 
     def drain(self):
-        sent = self.send.at[pl.ds(0, SLABS - 1)]
+        sent = self.recv.at[pl.ds(0, SLABS - 1)]
         pltpu.make_async_copy(sent, sent, self.ss).wait()
 
 
@@ -308,7 +316,8 @@
         osend=vm((SLABS, 8, 128), BF16), orecv=vm((SLABS, 8, 128), BF16),
         gsend=vm((SLABS, 8, 128), BF16), grecv=vm((SLABS, 8, 128), BF16),
         dsend=vm((SLABS, 8, 384), BF16), drecv=vm((SLABS, 8, 384), BF16),
-        ss_x=dma((4,)), rs_x=dma((4,)),
+        hsend=vm((16, 8, 512), BF16), hrecv=vm((SLABS, 8, 512), BF16),
+        ss_x=dma((5,)), rs_x=dma((5,)),
         z32=vm((3, 512, 128), F32), o32=vm((512, 128), F32), g32=vm((512, 128), F32), d32=vm((3, 512, 128), F32),
         px=vm((4, 128, 256), F32), py=vm((4, 128, 256), F32), pz=vm((4, 128, 256), F32),
         oxy=vm((128, 512), F32), dxy=vm((128, 1536), F32), gmix=vm((128, 512), BF16),
@@ -316,9 +325,10 @@
         b_h1=vm((256, 512), BF16), b_mixed=vm((256, 512), BF16), b_h2=vm((256, 512), BF16), b_act=vm((256, 2048), BF16),
         cot=vm((128, 512), BF16), gu=vm((128, 2048), BF16), grb=vm((128, 512), BF16), gp=vm((128, 1536), BF16),
         b_cot=vm((256, 256), BF16), b_gu=vm((256, 1024), BF16), b_grb=vm((256, 256), BF16), b_gp=vm((256, 768), BF16),
-        ss_core=dma((8,)), rs_core=dma((8,)),
-        down32=vm((SLABS, 32, 256), F32), gain32=vm((SLABS, 8, 128), F32),
-        one=sum_shapes(1280), two=sum_shapes(512),
+        ss_core=dma((10,)), rs_core=dma((10,)),
+        zpart=vm((512, 384), F32), zpart_b=vm((512, 384), BF16), zpeer=vm((2, 512, 128), BF16),
+        down32=vm((SLABS, 32, 256), F32), out32=vm((512, 256), F32), qkv32=vm((512, 768), F32),
+        one=sum_shapes(1024, True), two=sum_shapes(512, False),
     )
 
 
@@ -354,7 +364,9 @@
     gain_one, gain_two = ga[...], gm[...]
     r.flat[...] = to_rows(tok[...].astype(F32))
     normed_one, inverse_one = norm_stats(r.flat[...])
-    r.b_h1[0:128, :] = (normed_one * gain_one).astype(BF16)
+    hidden_one = normed_one * gain_one
+    r.b_h1[0:128, :] = hidden_one.astype(BF16)
+    r.hsend[...] = hidden_one.reshape(16, 8, 512).astype(BF16)
     r.cot[...] = to_rows(cot[...].astype(F32)).astype(BF16)
     loads[0].wait()
     for i in range(3):
@@ -368,6 +380,7 @@
     ex_o = Exchange(r.osend, r.orecv, r.ss_x.at[1], r.rs_x.at[1])
     ex_g = Exchange(r.gsend, r.grecv, r.ss_x.at[2], r.rs_x.at[2])
     ex_d = Exchange(r.dsend, r.drecv, r.ss_x.at[3], r.rs_x.at[3])
+    ex_h = Exchange(r.hsend, r.hrecv, r.ss_x.at[4], r.rs_x.at[4], shared=4)
     ex_q.start()
 
     core_copies = []
@@ -398,6 +411,11 @@
         r.py[j] = line_probs(scores, mask_y)
         r.oxy[:, 128 * j : 128 * j + 128] = pair_out((r.px[j] + r.py[j]).astype(BF16), values)
 
+    loads[2].wait()
+    for i in range(4):
+        at = slice(512 * i, 512 * i + 512)
+        r.gact[:, at] = nt(r.cot[...], r.wd[at, :])
+
     ex_q.wait()
     for i in range(3):
         r.z32[i] = r.qrecv[:, :, 128 * i : 128 * i + 128].astype(F32).reshape(512, 128)
@@ -412,10 +430,7 @@
         r.o32[pl.ds(j, 128, stride=4), :] = pair_out(probs.astype(BF16), values)
     r.osend[...] = r.o32[...].reshape(SLABS, 8, 128).astype(BF16)
     ex_o.start()
-    loads[2].wait()
-    for i in range(4):
-        at = slice(512 * i, 512 * i + 512)
-        r.gact[:, at] = nt(r.cot[...], r.wd[at, :])
+    ex_h.start()
 
     loads[1].wait()
     loads[3].wait()
@@ -448,8 +463,19 @@
     to_core_full(r.b_h2)
     to_core_full(r.b_mixed)
     to_core_half(r.grb, r.b_grb)
-    ones = jnp.ones((128, 128), BF16)
-    r.gain32[...] = tn((grad_hidden_two * normed_two).astype(BF16), ones).reshape(SLABS, 8, 128)
+
+    for j in range(4):
+        queries, keys, values = pair(j)
+        grads = r.gmix[:, 128 * j : 128 * j + 128]
+        grad_probs = nt(values, two_heads(grads))
+        probs_x, probs_y = r.px[j], r.py[j]
+        grad_scores = (score_grads(probs_x, grad_probs) + score_grads(probs_y, grad_probs)).astype(BF16)
+        back = pair_back((probs_x + probs_y).astype(BF16), grad_scores, queries, keys, grads)
+        for i in range(3):
+            at = slice(512 * i + 128 * j, 512 * i + 128 * j + 128)
+            r.dxy[:, at] = back[i]
+            r.gp[:, at] = back[i].astype(BF16)
+    to_core_half(r.gp, r.b_gp)
 
     one, two = Sum(r_one), Sum(r_two)
     for copy in core_copies:
@@ -463,10 +489,11 @@
         )
     one.put(512, r.down32[:, 0:8, :], r.down32[:, 16:24, :])
     one.put(768, r.down32[:, 8:16, :], r.down32[:, 24:32, :])
-    upper = tn(r.b_mixed[...], r.b_grb[...]).reshape(SLABS, 8, 256)
-    one.put(1024, upper[:, :, 0:128], r.gain32[...])
-    one.put(1152, upper[:, :, 128:256], jnp.zeros((SLABS, 8, 128), F32))
     one.start()
+    r.out32[...] = tn(r.b_mixed[...], r.b_grb[...])
+    for i in range(3):
+        at = slice(256 * i, 256 * i + 256)
+        r.qkv32[:, at] = tn(r.b_h1[...], r.b_gp[:, at])
 
     ex_g.wait()
     r.g32[...] = r.grecv[...].astype(F32).reshape(512, 128)
@@ -478,50 +505,63 @@
         back = pair_back(probs.astype(BF16), grad_scores, queries, keys, grads)
         for i in range(3):
             r.d32[i, pl.ds(j, 128, stride=4), :] = back[i]
+
+    ex_h.wait()
+    hidden_lines = r.hrecv[...].astype(F32).reshape(512, 512).astype(BF16)
+    r.zpart[...] = tn(hidden_lines, jnp.concatenate([r.d32[i].astype(BF16) for i in range(3)], axis=1))
+    r.zpart_b[...] = r.zpart[...].astype(BF16)
+
+    def outer(owner):
+        return pl.ds(pl.multiple_of(owner * 256, 128), 128)
+
+    z_copies = [
+        remote(r.zpart_b.at[:, outer(1 - core)], r.zpeer.at[0], r.ss_core.at[8], r.rs_core.at[8], other),
+        remote(r.zpart_b.at[:, pl.ds(128, 128)], r.zpeer.at[1], r.ss_core.at[9], r.rs_core.at[9], other),
+    ]
+    one.middle()
     for i in range(3):
         r.dsend[:, :, 128 * i : 128 * i + 128] = r.d32[i].reshape(SLABS, 8, 128).astype(BF16)
+    pair_at = slab % 4
+    at_outer = pl.ds(pl.multiple_of(core * 256 + pair_at * 128, 128), 128)
+    at_keys = pl.ds(pl.multiple_of((1 - core) * 512 + (pair_at % 2) * 128, 128), 128)
+    owned = jnp.where(core == pair_at // 2, 1.0, 0.0)
+    z_copies[0].wait_recv()
+    r.qkv32[:, at_outer] = r.qkv32[:, at_outer] + (r.zpart[:, outer(core)] + r.zpeer[0].astype(F32))
+    z_copies[1].wait_recv()
+    r.qkv32[:, at_keys] = r.qkv32[:, at_keys] + owned * (r.zpart[:, 128:256] + r.zpeer[1].astype(F32))
+
+    def rows(ref, at):
+        return ref[:, at : at + 256].reshape(SLABS, 8, 256)
+
+    two.put(0, rows(r.qkv32, 0), rows(r.qkv32, 256))
+    two.put(256, rows(r.qkv32, 512), rows(r.out32, 0))
+    two.start()
     ex_d.start()
-
-    for j in range(4):
-        queries, keys, values = pair(j)
-        grads = r.gmix[:, 128 * j : 128 * j + 128]
-        grad_probs = nt(values, two_heads(grads))
-        probs_x, probs_y = r.px[j], r.py[j]
-        grad_scores = (score_grads(probs_x, grad_probs) + score_grads(probs_y, grad_probs)).astype(BF16)
-        back = pair_back((probs_x + probs_y).astype(BF16), grad_scores, queries, keys, grads)
-        for i in range(3):
-            r.dxy[:, 512 * i + 128 * j : 512 * i + 128 * j + 128] = back[i]
-
-    one.middle()
+    one.second()
+    two.second()
+    one.along_z()
+    two.along_z()
 
     ex_d.wait()
     for i in range(3):
         from_z = r.drecv[:, :, 128 * i : 128 * i + 128].astype(F32).reshape(16, 4, 8, 128)
         for j in range(4):
             at = slice(512 * i + 128 * j, 512 * i + 128 * j + 128)
-            r.gp[:, at] = (r.dxy[:, at] + from_z[:, j].reshape(128, 128)).astype(BF16)
-    to_core_half(r.gp, r.b_gp)
-    grad_hidden_one = nt(r.gp[...], r.wq[...])
+            r.dxy[:, at] = r.dxy[:, at] + from_z[:, j].reshape(128, 128)
+    grad_hidden_one = nt(r.dxy[...].astype(BF16), r.wq[...])
     normed_one, inverse_one = norm_stats(r.flat[...])
     first, second = to_grid(r.gres[...] + norm_back(grad_hidden_one, normed_one, inverse_one, gain_one))
     o_tok[0] = first.astype(BF16)
     o_tok[1] = second.astype(BF16)
-    gains = tn((grad_hidden_one * normed_one).astype(BF16), ones).reshape(SLABS, 8, 128)
-    one.second()
-    core_copies[-1].wait_recv()
-    parts = [tn(r.b_h1[...], r.b_gp[:, 256 * i : 256 * i + 256]).reshape(SLABS, 8, 256) for i in range(3)]
-    two.put(0, parts[0], parts[2])
-    two.put(256, parts[1][:, :, 0:128], gains)
-    two.put(384, parts[1][:, :, 128:256], jnp.zeros((SLABS, 8, 128), F32))
-    two.start()
-    one.second_middle()
-    two.middle()
-    one.along_z()
-    two.second()
+
     one.gather()
-    two.second_middle()
-    two.along_z()
-    gain = jnp.zeros((8, 128), F32)
+    two.gather()
+    own_rows = pl.ds(pl.multiple_of((slab // 2) * 16, 16), 16)
+
+    def weight_rows(ref):
+        both = ref[own_rows, :].astype(F32)
+        return jnp.where(slab % 2 == 0, both[0:8], both[8:16])
+
     for c, full in enumerate(one.finish()):
         full = full * factor
         o_up[:, 1024 * c : 1024 * c + 512] = full[0:8, 0:512]
@@ -531,24 +571,30 @@
         o_down[8:16, at] = full[0:8, 768:1024]
         o_down[16:24, at] = full[8:16, 512:768]
         o_down[24:32, at] = full[8:16, 768:1024]
-        o_out[:, at] = full[0:8, 1024:1280]
-        gain = gain + full[8:16, 1024:1152]
-    o_g2[...] = gain
-    two.gather()
-    gain = jnp.zeros((8, 128), F32)
+    o_g2[...] = jnp.broadcast_to(jnp.sum(o_up[...] * weight_rows(r.wu), axis=1, keepdims=True), (8, 128))
     for c, full in enumerate(two.finish()):
         full = full * factor
-        o_qkv[:, 768 * c : 768 * c + 512] = full[0:8, 0:512]
-        o_qkv[:, 768 * c + 512 : 768 * c + 768] = full[8:16, 0:256]
-        gain = gain + full[8:16, 256:384]
-    o_g1[...] = gain
-
-    for exchange in (ex_q, ex_o, ex_g, ex_d):
+        o_qkv[:, 768 * c : 768 * c + 256] = full[0:8, 0:256]
+        o_qkv[:, 768 * c + 256 : 768 * c + 512] = full[8:16, 0:256]
+        o_qkv[:, 768 * c + 512 : 768 * c + 768] = full[0:8, 256:512]
+        o_out[:, 256 * c : 256 * c + 256] = full[8:16, 256:512]
+    o_g1[...] = jnp.broadcast_to(jnp.sum(o_qkv[...] * weight_rows(r.wq), axis=1, keepdims=True), (8, 128))
+
+    for exchange in (ex_q, ex_o, ex_h, ex_g, ex_d):
         exchange.drain()
-    for copy in core_copies:
+    for copy in core_copies + z_copies:
         copy.wait_send()
     one.drain()
     two.drain()
+
+
+def results_kernel(tok, qkv, out, up, down, g1, g2, gain_one, gain_two, o_tok, o_qkv, o_out, o_up, o_down, o_g1, o_g2):
+    for src, dst in ((tok, o_tok), (qkv, o_qkv), (out, o_out), (up, o_up), (down, o_down)):
+        dst[...] = src[...]
+    row = lax.broadcasted_iota(jnp.int32, (8, 128), 0)
+    lane = lax.broadcasted_iota(jnp.int32, (8, 128), 1)
+    for src, gain, dst in ((g1, gain_one, o_g1), (g2, gain_two, o_g2)):
+        dst[...] = jnp.sum(jnp.where(row == lane, src[...], 0.0), axis=0)[0:8] / gain[...]
 
 
 def body(tokens, cotangent, w_qkv, w_out, w_up, w_down, gain_attn, gain_mlp):
@@ -578,15 +624,16 @@
         gain_attn.reshape(1, width),
         gain_mlp.reshape(1, width),
     )
-    return (
-        result[0].reshape(tokens.shape),
-        result[1],
-        result[2],
-        result[3],
-        result[4],
-        result[5][:, 0],
-        result[6][:, 0],
-    )
+    first = lax.axis_index("slab") * 8
+    gains = [lax.dynamic_slice(g, (first,), (8,)) for g in (gain_attn, gain_mlp)]
+    result = pl.pallas_call(
+        results_kernel,
+        out_shape=[jax.ShapeDtypeStruct((2, 8, 8, width), BF16)]
+        + [jax.ShapeDtypeStruct(s, F32) for s in outs[:4] + ((8,), (8,))],
+        in_specs=[vmem] * 9,
+        out_specs=[vmem] * 7,
+    )(*result, *gains)
+    return (result[0].reshape(tokens.shape), *result[1:])
 
 
 def solution(mesh):

time: 96.7 us -> 85.4 us (0.88)
  local copies, waits for them, and re-layouts: 8.63 us -> 2.61 us
  Pallas kernels: 87.1 us -> 82 us
    unnamed x5 -> x0, local copies, waits for them, and re-layouts: 7.25 us -> none
    pallas_call x1, Pallas kernels: 87.1 us -> 80.3 us  [body(): pl.pallas_call(functools.partial(kernel, factor, tree), out_shape=[jax.Sh...]
    dynamic_slice x0 -> x2, local copies, waits for them, and re-layouts: none -> 2.61 us  [body(): lax.dynamic_slice(g, (first,), (8,))]
    pallas_call x0 -> x1, Pallas kernels: none -> 1.72 us  [body(): pl.pallas_call(results_kernel, out_shape=[jax.ShapeDtypeStruct((2, 8, 8,...]
    slice x1 -> x0, local copies, waits for them, and re-layouts: 1.38 us -> none  [body(): result[6][:, 0]]
where the time goes in v3:
time: 85.4 us; the launch traced here: 85.2 us
  Pallas kernels  82 us (96%)
  local copies, waits for them, and re-layouts  2.61 us (3%)
    pallas_call x1, Pallas kernels, body(): pl.pallas_call(functools.partial(kernel, factor, tree), out_shape=[jax.Sh...  80.3 us
    dynamic_slice x2, local copies, waits for them, and re-layouts, body(): lax.dynamic_slice(g, (first,), (8,))  2.61 us
    pallas_call x1, Pallas kernels, body(): pl.pallas_call(results_kernel, out_shape=[jax.ShapeDtypeStruct((2, 8, 8,...  1.72 us

profile of v3, /device:TPU:1, one launch (start us, length us, event | category | flops | bytes accessed | tf_op | source)
XLA Modules:
  0.0 85.2 jit_solution(6636311995340758290)
XLA Ops:
  0.6 1.3 %dynamic_slice.6.gain_one = f32[8]{0:T(128)} dynamic-slice(f32[512]{0:T(512)} %param.14, s32[]{:T(128)S(6)} %select_n.4), dynamic_slice_sizes={8} | dynamic-slice | bytes 68 | tf_op jit(solution)/shard_map/dynamic_slice | solution.py:628
  2.0 1.3 %dynamic_slice.7.gain_two = f32[8]{0:T(128)} dynamic-slice(f32[512]{0:T(512)} %param.15, s32[]{:T(128)S(6)} %select_n.4), dynamic_slice_sizes={8} | dynamic-slice | bytes 68 | tf_op jit(solution)/shard_map/dynamic_slice | solution.py:628
  3.2 80.3 %shard_map.135 = (bf16[2,8,8,512]{3,2,1,0:T(8,128)(2,1)}, f32[8,1536]{1,0:T(8,128)}, f32[8,512]{1,0:T(8,128)}, f32[8,2048]{1,0:T(8,128)}, f32[32,512]{1,0:T(8,128)}, /*index=5*/f32[8,128]{1,0:T(8,128)}, f32[8,128]{1,0:T(8,128)}) custom-call(bf16[2,8,8,512]{3,2,1,0:T(8,128)(2,1)} %bitcast.5, bf16[2,8,8,512]{3,2,1,0:T(8,128)(2,1)} %bitcast.6, ...), custom_call_target="tpu_custom_call" | custom-call | flops 3500000000 | bytes 7000000 | tf_op jit(solution)/shard_map/pallas_call | solution.py:607
  83.5 1.7 %shard_map.136 = (bf16[2,8,8,512]{3,2,1,0:T(8,128)(2,1)}, f32[8,1536]{1,0:T(8,128)}, f32[8,512]{1,0:T(8,128)}, f32[8,2048]{1,0:T(8,128)}, f32[32,512]{1,0:T(8,128)}, /*index=5*/f32[8]{0:T(128)}, f32[8]{0:T(128)}) custom-call(bf16[2,8,8,512]{3,2,1,0:T(8,128)(2,1)} %get-tuple-element.21.tok, f32[8,1536]{1,0:T(8,128)} %get-tuple-element.22.qkv, ...), custom_call_target="tpu_custom_call" | custom-call | tf_op jit(solution)/shard_map/pallas_call | solution.py:629

commit v4 on v3

--- a/solution.py
+++ b/solution.py
@@ -167,14 +167,16 @@
     shapes = dict(
         buf=vm((4, 8, 2, 16, wide), BF16),
         fin_a=vm((3, 2, 2, 2, 16, wide), BF16), fin_b=vm((3, 2, 2, 4, 16, part), BF16),
-        a1=vm((4, 2, 16, wide), BF16), b1=vm((4, 4, 16, part), BF16),
-        fin_a2=vm((3, 2, 2, 16, part), BF16), fin_b2=vm((3, 2, 2, 16, part), BF16),
-        zbuf=vm((8, 16, part), BF16), zrecv=vm((7, 16, part), BF16), gath=vm((4, 16, part), BF16),
-        ss_ring=dma((4, 6)), rs_ring=dma((4, 6)), ss_z=dma((7,)), rs_z=dma((7,)), ss_g=dma((3,)), rs_g=dma((3,)),
+        cbuf=vm((8, 4, 16, part), BF16), crecv=vm((32, 16, part), BF16), gath=vm((4, 16, part), BF16),
+        ss_ring=dma((2, 6)), rs_ring=dma((2, 6)), ss_c=dma((1,)), rs_c=dma((1,)), ss_g=dma((3,)), rs_g=dma((3,)),
     )
     if relays:
         shapes.update(relay_a=vm((2, 2, 2, 16, wide), BF16), relay_b=vm((2, 2, 4, 16, part), BF16))
     return shapes
+
+
+def far_first(k, half):
+    return half + ((k + 1) // 2) * (1 - 2 * (k % 2))
 
 
 class Sum:
@@ -183,7 +185,7 @@
         x, z, y_hi, y_lo, core = places()
         self.place = (x, z, y_hi, y_lo, core)
         y = y_hi * 2 + y_lo
-        part = ref.zbuf.shape[-1]
+        part = ref.gath.shape[-1]
 
         def lanes(lo):
             return pl.ds(pl.multiple_of(lo * part, 128), part)
@@ -194,18 +196,13 @@
         def dev_y(i):
             return device(x, z, i // 2, i % 2, core)
 
-        sems = [(ref.ss_ring.at[i], ref.rs_ring.at[i]) for i in range(4)]
+        sems = [(ref.ss_ring.at[i], ref.rs_ring.at[i]) for i in range(2)]
         relay_a, relay_b = getattr(ref, "relay_a", None), getattr(ref, "relay_b", None)
         self.a = Ring(x, dev_x, lambda i, h: ref.buf.at[i, pl.ds(2 * h, 2)], relay_a, ref.fin_a, *sems[0])
         self.b = Ring(
             y, dev_y, lambda i, h: ref.buf.at[pl.ds(2 * h, 2), pl.ds(4, 4), i // 2, :, lanes(i % 2)],
             relay_b, ref.fin_b, *sems[1],
         )
-        self.a2 = Ring(
-            y, dev_y, lambda i, h: ref.a1.at[pl.ds(2 * h, 2), i // 2, :, lanes(i % 2)],
-            None, ref.fin_a2, *sems[2],
-        )
-        self.b2 = Ring(x, dev_x, lambda i, h: ref.b1.at[i, pl.ds(2 * h, 2)], None, ref.fin_b2, *sems[3])
         self.copies = []
 
     def put(self, at, upper, lower):
@@ -222,55 +219,68 @@
         self.b.middle()
 
     def second(self):
+        ref = self.ref
+        x, z, y_hi, y_lo, core = self.place
+        y = y_hi * 2 + y_lo
+        part = ref.gath.shape[-1]
         self.a.finish()
         for h in range(2):
-            self.ref.a1[2 * h : 2 * h + 2] = self.a.result(h)
-        self.a2.start()
+            done = self.a.result(h)
+            for i in range(4):
+                ref.cbuf[2 * h : 2 * h + 2, i] = done[:, i // 2, :, (i % 2) * part : (i % 2) * part + part]
         self.b.finish()
         for h in range(2):
-            self.ref.b1[2 * h : 2 * h + 2] = self.b.result(h)
-        self.b2.start()
-
-    def along_z(self):
-        ref = self.ref
-        x, z, y_hi, y_lo, core = self.place
-        self.a2.finish()
-        for h in range(2):
-            ref.zbuf[2 * h : 2 * h + 2] = self.a2.result(h)
-        self.b2.finish()
-        for h in range(2):
-            ref.zbuf[4 + 2 * h : 6 + 2 * h] = self.b2.result(h)
-        for d in range(1, 8):
-            to = (z + d) % 8
-            self.copies.append(
-                remote(ref.zbuf.at[to], ref.zrecv.at[d - 1], ref.ss_z.at[d - 1], ref.rs_z.at[d - 1],
-                       device(x, to, y_hi, y_lo, core))
-            )
+            done = self.b.result(h)
+            for i in range(2):
+                ref.cbuf[4:8, 2 * h + i] = done[i]
+
+        def one(n, carry):
+            to_z = (z + far_first(n // 4, 4)) % 8
+            step = far_first(n % 4, 2)
+            low = 1 - to_z // 4
+            to = low * ((y + step) % 4) + (1 - low) * ((x + step) % 4)
+            to_x, to_y = low * x + (1 - low) * to, low * to + (1 - low) * y
+            remote(ref.cbuf.at[to_z, to], ref.crecv.at[z * 4 + low * y + (1 - low) * x], ref.ss_c.at[0], ref.rs_c.at[0],
+                   device(to_x, to_z, to_y // 2, to_y % 2, core))
+            return carry
+
+        lax.fori_loop(0, 31, one, 0)
+        low = 1 - z // 4
+        own = low * y + (1 - low) * x
+        ref.crecv[z * 4 + own] = ref.cbuf[z, own]
 
     def gather(self):
         ref = self.ref
         x, z, y_hi, y_lo, core = self.place
-        total = ref.zbuf[z].astype(F32)
-        for d in range(7):
-            self.copies[d].wait_recv()
-            total = total + ref.zrecv[d].astype(F32)
+        got = ref.crecv.at[pl.ds(0, 31)]
+        pltpu.make_async_copy(got, got, ref.rs_c.at[0]).wait()
         mine = y_lo * 2 + core
-        ref.gath[mine] = total.astype(BF16)
-        for n, (dy, dc) in enumerate(((0, 1), (1, 0), (1, 1))):
-            to = device(x, z, y_hi, (y_lo + dy) % 2, (core + dc) % 2)
-            self.copies.append(remote(ref.gath.at[mine], ref.gath.at[mine], ref.ss_g.at[n], ref.rs_g.at[n], to))
+        ref.gath[mine] = jnp.sum(ref.crecv[...].astype(F32), axis=0).astype(BF16)
+        self.copies = share(ref.gath, ref.ss_g, ref.rs_g)
 
     def finish(self):
-        for copy in self.copies[7:]:
+        for copy in self.copies:
             copy.wait_recv()
         gath = self.ref.gath
         return [jnp.concatenate([gath[c].astype(F32), gath[2 + c].astype(F32)], axis=1) for c in range(2)]
 
     def drain(self):
+        sent = self.ref.crecv.at[pl.ds(0, 31)]
+        pltpu.make_async_copy(sent, sent, self.ref.ss_c.at[0]).wait()
         for copy in self.copies:
             copy.wait_send()
-        for ring in (self.a, self.b, self.a2, self.b2):
+        for ring in (self.a, self.b):
             ring.drain()
+
+
+def share(ref, send_sem, recv_sem):
+    x, z, y_hi, y_lo, core = places()
+    mine = y_lo * 2 + core
+    return [
+        remote(ref.at[mine], ref.at[mine], send_sem.at[n], recv_sem.at[n],
+               device(x, z, y_hi, (y_lo + dy) % 2, (core + dc) % 2))
+        for n, (dy, dc) in enumerate(((1, 1), (1, 0), (0, 1)))
+    ]
 
 
 class Exchange:
@@ -283,8 +293,7 @@
 
         def one(n, carry):
             kz, kx, ky = n // 8, (n // 2) % 4, n % 2
-            dz = 4 + ((kz + 1) // 2) * (1 - 2 * (kz % 2))
-            dx = 2 + ((kx + 1) // 2) * (1 - 2 * (kx % 2))
+            dz, dx = far_first(kz, 4), far_first(kx, 2)
             to = device((x + dx) % 4, (z + dz) % 8, (y_hi + 1 - ky) % 2, y_lo, core)
             remote(self.send.at[to[0] // self.shared], self.recv.at[me], self.ss, self.rs, to)
             return carry
@@ -317,7 +326,8 @@
         gsend=vm((SLABS, 8, 128), BF16), grecv=vm((SLABS, 8, 128), BF16),
         dsend=vm((SLABS, 8, 384), BF16), drecv=vm((SLABS, 8, 384), BF16),
         hsend=vm((16, 8, 512), BF16), hrecv=vm((SLABS, 8, 512), BF16),
-        ss_x=dma((5,)), rs_x=dma((5,)),
+        psend=vm((SLABS, 8, 384), BF16), precv=vm((SLABS, 8, 384), BF16), pgath=vm((4, 8, 1536), BF16),
+        ss_x=dma((6,)), rs_x=dma((6,)), ss_p=dma((3,)), rs_p=dma((3,)),
         z32=vm((3, 512, 128), F32), o32=vm((512, 128), F32), g32=vm((512, 128), F32), d32=vm((3, 512, 128), F32),
         px=vm((4, 128, 256), F32), py=vm((4, 128, 256), F32), pz=vm((4, 128, 256), F32),
         oxy=vm((128, 512), F32), dxy=vm((128, 1536), F32), gmix=vm((128, 512), BF16),
@@ -325,9 +335,8 @@
         b_h1=vm((256, 512), BF16), b_mixed=vm((256, 512), BF16), b_h2=vm((256, 512), BF16), b_act=vm((256, 2048), BF16),
         cot=vm((128, 512), BF16), gu=vm((128, 2048), BF16), grb=vm((128, 512), BF16), gp=vm((128, 1536), BF16),
         b_cot=vm((256, 256), BF16), b_gu=vm((256, 1024), BF16), b_grb=vm((256, 256), BF16), b_gp=vm((256, 768), BF16),
-        ss_core=dma((10,)), rs_core=dma((10,)),
-        zpart=vm((512, 384), F32), zpart_b=vm((512, 384), BF16), zpeer=vm((2, 512, 128), BF16),
-        down32=vm((SLABS, 32, 256), F32), out32=vm((512, 256), F32), qkv32=vm((512, 768), F32),
+        ss_core=dma((8,)), rs_core=dma((8,)),
+        down32=vm((SLABS, 32, 256), F32),
         one=sum_shapes(1024, True), two=sum_shapes(512, False),
     )
 
@@ -353,12 +362,13 @@
         return carry
 
     lax.fori_loop(1, SLABS, greet, 0)
-    for peer in (
-        other,
-        device(x, z, y_hi, 1 - y_lo, core),
-        device(x, z, y_hi, 1 - y_lo, 1 - core),
-        device(x, z, 1 - y_hi, 1 - y_lo, core),
-    ):
+    def greet_y(n, carry):
+        peer = device(x, n // 2, n % 2, 1 - y_lo, core)
+        pl.semaphore_signal(barrier, inc=1, device_id=peer, device_id_type=MESH)
+        return carry
+
+    lax.fori_loop(0, 16, greet_y, 0)
+    for peer in (other, device(x, z, y_hi, 1 - y_lo, 1 - core)):
         pl.semaphore_signal(barrier, inc=1, device_id=peer, device_id_type=MESH)
 
     gain_one, gain_two = ga[...], gm[...]
@@ -375,12 +385,13 @@
         r.qsend[:, :, 128 * i : 128 * i + 128] = by_pair(
             [r.qkv[:, 512 * i + 128 * j : 512 * i + 128 * j + 128].astype(F32) for j in range(4)]
         ).astype(BF16)
-    pl.semaphore_wait(barrier, SLABS + 3)
+    pl.semaphore_wait(barrier, SLABS - 1 + 16 + 2)
     ex_q = Exchange(r.qsend, r.qrecv, r.ss_x.at[0], r.rs_x.at[0])
     ex_o = Exchange(r.osend, r.orecv, r.ss_x.at[1], r.rs_x.at[1])
     ex_g = Exchange(r.gsend, r.grecv, r.ss_x.at[2], r.rs_x.at[2])
     ex_d = Exchange(r.dsend, r.drecv, r.ss_x.at[3], r.rs_x.at[3])
     ex_h = Exchange(r.hsend, r.hrecv, r.ss_x.at[4], r.rs_x.at[4], shared=4)
+    ex_p = Exchange(r.psend, r.precv, r.ss_x.at[5], r.rs_x.at[5])
     ex_q.start()
 
     core_copies = []
@@ -464,6 +475,20 @@
     to_core_full(r.b_mixed)
     to_core_half(r.grb, r.b_grb)
 
+    one, two = Sum(r_one), Sum(r_two)
+    for copy in core_copies[1:5]:
+        copy.wait_recv()
+    r.down32[...] = tn(r.b_act[...], r.b_cot[...]).reshape(SLABS, 32, 256)
+    for i in range(2):
+        one.put(
+            256 * i,
+            tn(r.b_h2[...], r.b_gu[:, 256 * i : 256 * i + 256]).reshape(SLABS, 8, 256),
+            tn(r.b_h2[...], r.b_gu[:, 512 + 256 * i : 768 + 256 * i]).reshape(SLABS, 8, 256),
+        )
+    one.put(512, r.down32[:, 0:8, :], r.down32[:, 16:24, :])
+    one.put(768, r.down32[:, 8:16, :], r.down32[:, 24:32, :])
+    one.start()
+
     for j in range(4):
         queries, keys, values = pair(j)
         grads = r.gmix[:, 128 * j : 128 * j + 128]
@@ -477,23 +502,15 @@
             r.gp[:, at] = back[i].astype(BF16)
     to_core_half(r.gp, r.b_gp)
 
-    one, two = Sum(r_one), Sum(r_two)
-    for copy in core_copies:
+    for copy in core_copies[0:1] + core_copies[5:]:
         copy.wait_recv()
-    r.down32[...] = tn(r.b_act[...], r.b_cot[...]).reshape(SLABS, 32, 256)
-    for i in range(2):
-        one.put(
-            256 * i,
-            tn(r.b_h2[...], r.b_gu[:, 256 * i : 256 * i + 256]).reshape(SLABS, 8, 256),
-            tn(r.b_h2[...], r.b_gu[:, 512 + 256 * i : 768 + 256 * i]).reshape(SLABS, 8, 256),
-        )
-    one.put(512, r.down32[:, 0:8, :], r.down32[:, 16:24, :])
-    one.put(768, r.down32[:, 8:16, :], r.down32[:, 24:32, :])
-    one.start()
-    r.out32[...] = tn(r.b_mixed[...], r.b_grb[...])
-    for i in range(3):
-        at = slice(256 * i, 256 * i + 256)
-        r.qkv32[:, at] = tn(r.b_h1[...], r.b_gp[:, at])
+
+    def qkv_part(i):
+        return tn(r.b_h1[...], r.b_gp[:, 256 * i : 256 * i + 256]).reshape(SLABS, 8, 256)
+
+    two.put(0, qkv_part(0), qkv_part(1))
+    two.put(256, qkv_part(2), tn(r.b_mixed[...], r.b_grb[...]).reshape(SLABS, 8, 256))
+    two.start()
 
     ex_g.wait()
     r.g32[...] = r.grecv[...].astype(F32).reshape(512, 128)
@@ -508,39 +525,23 @@
 
     ex_h.wait()
     hidden_lines = r.hrecv[...].astype(F32).reshape(512, 512).astype(BF16)
-    r.zpart[...] = tn(hidden_lines, jnp.concatenate([r.d32[i].astype(BF16) for i in range(3)], axis=1))
-    r.zpart_b[...] = r.zpart[...].astype(BF16)
-
-    def outer(owner):
-        return pl.ds(pl.multiple_of(owner * 256, 128), 128)
-
-    z_copies = [
-        remote(r.zpart_b.at[:, outer(1 - core)], r.zpeer.at[0], r.ss_core.at[8], r.rs_core.at[8], other),
-        remote(r.zpart_b.at[:, pl.ds(128, 128)], r.zpeer.at[1], r.ss_core.at[9], r.rs_core.at[9], other),
-    ]
+    for i in range(3):
+        r.psend[:, :, 128 * i : 128 * i + 128] = tn(hidden_lines, r.d32[i].astype(BF16)).reshape(SLABS, 8, 128).astype(BF16)
+    ex_p.start()
     one.middle()
     for i in range(3):
         r.dsend[:, :, 128 * i : 128 * i + 128] = r.d32[i].reshape(SLABS, 8, 128).astype(BF16)
-    pair_at = slab % 4
-    at_outer = pl.ds(pl.multiple_of(core * 256 + pair_at * 128, 128), 128)
-    at_keys = pl.ds(pl.multiple_of((1 - core) * 512 + (pair_at % 2) * 128, 128), 128)
-    owned = jnp.where(core == pair_at // 2, 1.0, 0.0)
-    z_copies[0].wait_recv()
-    r.qkv32[:, at_outer] = r.qkv32[:, at_outer] + (r.zpart[:, outer(core)] + r.zpeer[0].astype(F32))
-    z_copies[1].wait_recv()
-    r.qkv32[:, at_keys] = r.qkv32[:, at_keys] + owned * (r.zpart[:, 128:256] + r.zpeer[1].astype(F32))
-
-    def rows(ref, at):
-        return ref[:, at : at + 256].reshape(SLABS, 8, 256)
-
-    two.put(0, rows(r.qkv32, 0), rows(r.qkv32, 256))
-    two.put(256, rows(r.qkv32, 512), rows(r.out32, 0))
-    two.start()
     ex_d.start()
+    two.second()
     one.second()
-    two.second()
-    one.along_z()
-    two.along_z()
+    ex_p.wait()
+    lines = jnp.sum(r.precv[...].astype(F32).reshape(16, 4, 8, 384), axis=0).astype(BF16)
+    case_at = y_lo * 2 + core
+    for i in range(3):
+        for j in range(4):
+            at = 512 * i + 128 * j
+            r.pgath[case_at, :, at : at + 128] = lines[j, :, 128 * i : 128 * i + 128]
+    p_copies = share(r.pgath, r.ss_p, r.rs_p)
 
     ex_d.wait()
     for i in range(3):
@@ -554,8 +555,8 @@
     o_tok[0] = first.astype(BF16)
     o_tok[1] = second.astype(BF16)
 
+    two.gather()
     one.gather()
-    two.gather()
     own_rows = pl.ds(pl.multiple_of((slab // 2) * 16, 16), 16)
 
     def weight_rows(ref):
@@ -571,30 +572,40 @@
         o_down[8:16, at] = full[0:8, 768:1024]
         o_down[16:24, at] = full[8:16, 512:768]
         o_down[24:32, at] = full[8:16, 768:1024]
-    o_g2[...] = jnp.broadcast_to(jnp.sum(o_up[...] * weight_rows(r.wu), axis=1, keepdims=True), (8, 128))
+
+    def over_gain(rows, gain):
+        lane = lax.broadcasted_iota(jnp.int32, (8, 512), 1)
+        row = lax.broadcasted_iota(jnp.int32, (8, 512), 0)
+        own = jnp.sum(jnp.where(lane == slab * 8 + row, gain, 0.0), axis=1, keepdims=True)
+        return jnp.broadcast_to(jnp.sum(rows, axis=1, keepdims=True) / own, (8, 128))
+
+    o_g2[...] = over_gain(o_up[...] * weight_rows(r.wu), gain_two)
+    for copy in p_copies:
+        copy.wait_recv()
+    o_qkv[...] = jnp.sum(r.pgath[...].astype(F32), axis=0) * factor
     for c, full in enumerate(two.finish()):
         full = full * factor
-        o_qkv[:, 768 * c : 768 * c + 256] = full[0:8, 0:256]
-        o_qkv[:, 768 * c + 256 : 768 * c + 512] = full[8:16, 0:256]
-        o_qkv[:, 768 * c + 512 : 768 * c + 768] = full[0:8, 256:512]
+        o_qkv[:, 768 * c : 768 * c + 256] += full[0:8, 0:256]
+        o_qkv[:, 768 * c + 256 : 768 * c + 512] += full[8:16, 0:256]
+        o_qkv[:, 768 * c + 512 : 768 * c + 768] += full[0:8, 256:512]
         o_out[:, 256 * c : 256 * c + 256] = full[8:16, 256:512]
-    o_g1[...] = jnp.broadcast_to(jnp.sum(o_qkv[...] * weight_rows(r.wq), axis=1, keepdims=True), (8, 128))
-
-    for exchange in (ex_q, ex_o, ex_h, ex_g, ex_d):
+    o_g1[...] = over_gain(o_qkv[...] * weight_rows(r.wq), gain_one)
+
+    for exchange in (ex_q, ex_o, ex_h, ex_g, ex_p, ex_d):
         exchange.drain()
-    for copy in core_copies + z_copies:
+    for copy in core_copies + p_copies:
         copy.wait_send()
     one.drain()
     two.drain()
 
 
-def results_kernel(tok, qkv, out, up, down, g1, g2, gain_one, gain_two, o_tok, o_qkv, o_out, o_up, o_down, o_g1, o_g2):
+def results_kernel(tok, qkv, out, up, down, g1, g2, o_tok, o_qkv, o_out, o_up, o_down, o_g1, o_g2):
     for src, dst in ((tok, o_tok), (qkv, o_qkv), (out, o_out), (up, o_up), (down, o_down)):
         dst[...] = src[...]
     row = lax.broadcasted_iota(jnp.int32, (8, 128), 0)
     lane = lax.broadcasted_iota(jnp.int32, (8, 128), 1)
-    for src, gain, dst in ((g1, gain_one, o_g1), (g2, gain_two, o_g2)):
-        dst[...] = jnp.sum(jnp.where(row == lane, src[...], 0.0), axis=0)[0:8] / gain[...]
+    for src, dst in ((g1, o_g1), (g2, o_g2)):
+        dst[...] = jnp.sum(jnp.where(row == lane, src[...], 0.0), axis=0)[0:8]
 
 
 def body(tokens, cotangent, w_qkv, w_out, w_up, w_down, gain_attn, gain_mlp):
@@ -624,15 +635,13 @@
         gain_attn.reshape(1, width),
         gain_mlp.reshape(1, width),
     )
-    first = lax.axis_index("slab") * 8
-    gains = [lax.dynamic_slice(g, (first,), (8,)) for g in (gain_attn, gain_mlp)]
     result = pl.pallas_call(
         results_kernel,
         out_shape=[jax.ShapeDtypeStruct((2, 8, 8, width), BF16)]
         + [jax.ShapeDtypeStruct(s, F32) for s in outs[:4] + ((8,), (8,))],
-        in_specs=[vmem] * 9,
+        in_specs=[vmem] * 7,
         out_specs=[vmem] * 7,
-    )(*result, *gains)
+    )(*result)
     return (result[0].reshape(tokens.shape), *result[1:])
 
 

time: 85.4 us -> 93 us (1.089)
  Pallas kernels: 82 us -> 92.2 us
  local copies, waits for them, and re-layouts: 2.61 us -> 0 us
    pallas_call x1, Pallas kernels: 80.3 us -> 90.5 us  [body(): pl.pallas_call(functools.partial(kernel, factor, tree), out_shape=[jax.Sh...]
    dynamic_slice x2 -> x0, local copies, waits for them, and re-layouts: 2.61 us -> none  [body(): lax.dynamic_slice(g, (first,), (8,))]
where the time goes in v4:
time: 93 us; the launch traced here: 92.9 us
  Pallas kernels  92.2 us (99%)
    pallas_call x1, Pallas kernels, body(): pl.pallas_call(functools.partial(kernel, factor, tree), out_shape=[jax.Sh...  90.5 us

profile of v4, /device:TPU:1, one launch (start us, length us, event | category | flops | bytes accessed | tf_op | source)
XLA Modules:
  0.0 92.9 jit_solution(18316234705510691499)
XLA Ops:
  0.6 90.5 %shard_map.135 = (bf16[2,8,8,512]{3,2,1,0:T(8,128)(2,1)}, f32[8,1536]{1,0:T(8,128)}, f32[8,512]{1,0:T(8,128)}, f32[8,2048]{1,0:T(8,128)}, f32[32,512]{1,0:T(8,128)}, /*index=5*/f32[8,128]{1,0:T(8,128)}, f32[8,128]{1,0:T(8,128)}) custom-call(bf16[2,8,8,512]{3,2,1,0:T(8,128)(2,1)} %bitcast.5, bf16[2,8,8,512]{3,2,1,0:T(8,128)(2,1)} %bitcast.6, ...), custom_call_target="tpu_custom_call" | custom-call | flops 3500000000 | bytes 7000000 | tf_op jit(solution)/shard_map/pallas_call | solution.py:618
  91.1 1.7 %shard_map.136 = (bf16[2,8,8,512]{3,2,1,0:T(8,128)(2,1)}, f32[8,1536]{1,0:T(8,128)}, f32[8,512]{1,0:T(8,128)}, f32[8,2048]{1,0:T(8,128)}, f32[32,512]{1,0:T(8,128)}, /*index=5*/f32[8]{0:T(128)}, f32[8]{0:T(128)}) custom-call(bf16[2,8,8,512]{3,2,1,0:T(8,128)(2,1)} %get-tuple-element.21.tok, f32[8,1536]{1,0:T(8,128)} %get-tuple-element.22.qkv, ...), custom_call_target="tpu_custom_call" | custom-call | tf_op jit(solution)/shard_map/pallas_call | solution.py:638

commit v5 on v4

--- a/solution.py
+++ b/solution.py
@@ -167,16 +167,14 @@
     shapes = dict(
         buf=vm((4, 8, 2, 16, wide), BF16),
         fin_a=vm((3, 2, 2, 2, 16, wide), BF16), fin_b=vm((3, 2, 2, 4, 16, part), BF16),
-        cbuf=vm((8, 4, 16, part), BF16), crecv=vm((32, 16, part), BF16), gath=vm((4, 16, part), BF16),
-        ss_ring=dma((2, 6)), rs_ring=dma((2, 6)), ss_c=dma((1,)), rs_c=dma((1,)), ss_g=dma((3,)), rs_g=dma((3,)),
+        a1=vm((4, 2, 16, wide), BF16), b1=vm((4, 4, 16, part), BF16),
+        fin_a2=vm((3, 2, 2, 16, part), BF16), fin_b2=vm((3, 2, 2, 16, part), BF16),
+        zbuf=vm((8, 16, part), BF16), zrecv=vm((7, 16, part), BF16), gath=vm((4, 16, part), BF16),
+        ss_ring=dma((4, 6)), rs_ring=dma((4, 6)), ss_z=dma((7,)), rs_z=dma((7,)), ss_g=dma((3,)), rs_g=dma((3,)),
     )
     if relays:
         shapes.update(relay_a=vm((2, 2, 2, 16, wide), BF16), relay_b=vm((2, 2, 4, 16, part), BF16))
     return shapes
-
-
-def far_first(k, half):
-    return half + ((k + 1) // 2) * (1 - 2 * (k % 2))
 
 
 class Sum:
@@ -185,7 +183,7 @@
         x, z, y_hi, y_lo, core = places()
         self.place = (x, z, y_hi, y_lo, core)
         y = y_hi * 2 + y_lo
-        part = ref.gath.shape[-1]
+        part = ref.zbuf.shape[-1]
 
         def lanes(lo):
             return pl.ds(pl.multiple_of(lo * part, 128), part)
@@ -196,13 +194,18 @@
         def dev_y(i):
             return device(x, z, i // 2, i % 2, core)
 
-        sems = [(ref.ss_ring.at[i], ref.rs_ring.at[i]) for i in range(2)]
+        sems = [(ref.ss_ring.at[i], ref.rs_ring.at[i]) for i in range(4)]
         relay_a, relay_b = getattr(ref, "relay_a", None), getattr(ref, "relay_b", None)
         self.a = Ring(x, dev_x, lambda i, h: ref.buf.at[i, pl.ds(2 * h, 2)], relay_a, ref.fin_a, *sems[0])
         self.b = Ring(
             y, dev_y, lambda i, h: ref.buf.at[pl.ds(2 * h, 2), pl.ds(4, 4), i // 2, :, lanes(i % 2)],
             relay_b, ref.fin_b, *sems[1],
         )
+        self.a2 = Ring(
+            y, dev_y, lambda i, h: ref.a1.at[pl.ds(2 * h, 2), i // 2, :, lanes(i % 2)],
+            None, ref.fin_a2, *sems[2],
+        )
+        self.b2 = Ring(x, dev_x, lambda i, h: ref.b1.at[i, pl.ds(2 * h, 2)], None, ref.fin_b2, *sems[3])
         self.copies = []
 
     def put(self, at, upper, lower):
@@ -219,57 +222,52 @@
         self.b.middle()
 
     def second(self):
+        self.a.finish()
+        for h in range(2):
+            self.ref.a1[2 * h : 2 * h + 2] = self.a.result(h)
+        self.a2.start()
+        self.b.finish()
+        for h in range(2):
+            self.ref.b1[2 * h : 2 * h + 2] = self.b.result(h)
+        self.b2.start()
+
+    def along_z(self):
         ref = self.ref
         x, z, y_hi, y_lo, core = self.place
-        y = y_hi * 2 + y_lo
-        part = ref.gath.shape[-1]
-        self.a.finish()
+        self.a2.finish()
         for h in range(2):
-            done = self.a.result(h)
-            for i in range(4):
-                ref.cbuf[2 * h : 2 * h + 2, i] = done[:, i // 2, :, (i % 2) * part : (i % 2) * part + part]
-        self.b.finish()
+            ref.zbuf[2 * h : 2 * h + 2] = self.a2.result(h)
+        self.b2.finish()
         for h in range(2):
-            done = self.b.result(h)
-            for i in range(2):
-                ref.cbuf[4:8, 2 * h + i] = done[i]
-
-        def one(n, carry):
-            to_z = (z + far_first(n // 4, 4)) % 8
-            step = far_first(n % 4, 2)
-            low = 1 - to_z // 4
-            to = low * ((y + step) % 4) + (1 - low) * ((x + step) % 4)
-            to_x, to_y = low * x + (1 - low) * to, low * to + (1 - low) * y
-            remote(ref.cbuf.at[to_z, to], ref.crecv.at[z * 4 + low * y + (1 - low) * x], ref.ss_c.at[0], ref.rs_c.at[0],
-                   device(to_x, to_z, to_y // 2, to_y % 2, core))
-            return carry
-
-        lax.fori_loop(0, 31, one, 0)
-        low = 1 - z // 4
-        own = low * y + (1 - low) * x
-        ref.crecv[z * 4 + own] = ref.cbuf[z, own]
+            ref.zbuf[4 + 2 * h : 6 + 2 * h] = self.b2.result(h)
+        for d in range(1, 8):
+            to = (z + d) % 8
+            self.copies.append(
+                remote(ref.zbuf.at[to], ref.zrecv.at[d - 1], ref.ss_z.at[d - 1], ref.rs_z.at[d - 1],
+                       device(x, to, y_hi, y_lo, core))
+            )
 
     def gather(self):
         ref = self.ref
         x, z, y_hi, y_lo, core = self.place
-        got = ref.crecv.at[pl.ds(0, 31)]
-        pltpu.make_async_copy(got, got, ref.rs_c.at[0]).wait()
+        total = ref.zbuf[z].astype(F32)
+        for d in range(7):
+            self.copies[d].wait_recv()
+            total = total + ref.zrecv[d].astype(F32)
         mine = y_lo * 2 + core
-        ref.gath[mine] = jnp.sum(ref.crecv[...].astype(F32), axis=0).astype(BF16)
-        self.copies = share(ref.gath, ref.ss_g, ref.rs_g)
+        ref.gath[mine] = total.astype(BF16)
+        self.copies += share(ref.gath, ref.ss_g, ref.rs_g)
 
     def finish(self):
-        for copy in self.copies:
+        for copy in self.copies[7:]:
             copy.wait_recv()
         gath = self.ref.gath
         return [jnp.concatenate([gath[c].astype(F32), gath[2 + c].astype(F32)], axis=1) for c in range(2)]
 
     def drain(self):
-        sent = self.ref.crecv.at[pl.ds(0, 31)]
-        pltpu.make_async_copy(sent, sent, self.ref.ss_c.at[0]).wait()
         for copy in self.copies:
             copy.wait_send()
-        for ring in (self.a, self.b):
+        for ring in (self.a, self.b, self.a2, self.b2):
             ring.drain()
 
 
@@ -283,9 +281,16 @@
     ]
 
 
+def far_first(k, half):
+    return half + ((k + 1) // 2) * (1 - 2 * (k % 2))
+
+
 class Exchange:
-    def __init__(self, send, recv, ss, rs, shared=1):
-        self.send, self.recv, self.ss, self.rs, self.shared = send, recv, ss, rs, shared
+    def __init__(self, send, recv, ss, rs, parts=False):
+        self.send, self.recv, self.ss, self.rs, self.parts = send, recv, ss, rs, parts
+
+    def landing(self, to):
+        return self.recv.at[to % 4] if self.parts else self.recv
 
     def start(self):
         me = lax.axis_index("slab")
@@ -295,18 +300,18 @@
             kz, kx, ky = n // 8, (n // 2) % 4, n % 2
             dz, dx = far_first(kz, 4), far_first(kx, 2)
             to = device((x + dx) % 4, (z + dz) % 8, (y_hi + 1 - ky) % 2, y_lo, core)
-            remote(self.send.at[to[0] // self.shared], self.recv.at[me], self.ss, self.rs, to)
+            remote(self.send.at[to[0]], self.landing(to[0]).at[me], self.ss, self.rs, to)
             return carry
 
         lax.fori_loop(0, SLABS - 1, one, 0)
-        self.recv[me] = self.send[me // self.shared]
+        self.landing(me)[me] = self.send[me]
 
     def wait(self):
-        got = self.recv.at[pl.ds(0, SLABS - 1)]
+        got = self.send.at[pl.ds(0, SLABS - 1)]
         pltpu.make_async_copy(got, got, self.rs).wait()
 
     def drain(self):
-        sent = self.recv.at[pl.ds(0, SLABS - 1)]
+        sent = self.send.at[pl.ds(0, SLABS - 1)]
         pltpu.make_async_copy(sent, sent, self.ss).wait()
 
 
@@ -325,7 +330,7 @@
         osend=vm((SLABS, 8, 128), BF16), orecv=vm((SLABS, 8, 128), BF16),
         gsend=vm((SLABS, 8, 128), BF16), grecv=vm((SLABS, 8, 128), BF16),
         dsend=vm((SLABS, 8, 384), BF16), drecv=vm((SLABS, 8, 384), BF16),
-        hsend=vm((16, 8, 512), BF16), hrecv=vm((SLABS, 8, 512), BF16),
+        hsend=vm((SLABS, 8, 128), BF16), hline=vm((4, SLABS, 8, 128), BF16), ss_h=dma((3,)), rs_h=dma((3,)),
         psend=vm((SLABS, 8, 384), BF16), precv=vm((SLABS, 8, 384), BF16), pgath=vm((4, 8, 1536), BF16),
         ss_x=dma((6,)), rs_x=dma((6,)), ss_p=dma((3,)), rs_p=dma((3,)),
         z32=vm((3, 512, 128), F32), o32=vm((512, 128), F32), g32=vm((512, 128), F32), d32=vm((3, 512, 128), F32),
@@ -362,13 +367,12 @@
         return carry
 
     lax.fori_loop(1, SLABS, greet, 0)
-    def greet_y(n, carry):
-        peer = device(x, n // 2, n % 2, 1 - y_lo, core)
-        pl.semaphore_signal(barrier, inc=1, device_id=peer, device_id_type=MESH)
-        return carry
-
-    lax.fori_loop(0, 16, greet_y, 0)
-    for peer in (other, device(x, z, y_hi, 1 - y_lo, 1 - core)):
+    for peer in (
+        other,
+        device(x, z, y_hi, 1 - y_lo, core),
+        device(x, z, y_hi, 1 - y_lo, 1 - core),
+        device(x, z, 1 - y_hi, 1 - y_lo, core),
+    ):
         pl.semaphore_signal(barrier, inc=1, device_id=peer, device_id_type=MESH)
 
     gain_one, gain_two = ga[...], gm[...]
@@ -376,7 +380,7 @@
     normed_one, inverse_one = norm_stats(r.flat[...])
     hidden_one = normed_one * gain_one
     r.b_h1[0:128, :] = hidden_one.astype(BF16)
-    r.hsend[...] = hidden_one.reshape(16, 8, 512).astype(BF16)
+    r.hsend[...] = by_pair([hidden_one[:, 128 * j : 128 * j + 128] for j in range(4)]).astype(BF16)
     r.cot[...] = to_rows(cot[...].astype(F32)).astype(BF16)
     loads[0].wait()
     for i in range(3):
@@ -385,12 +389,12 @@
         r.qsend[:, :, 128 * i : 128 * i + 128] = by_pair(
             [r.qkv[:, 512 * i + 128 * j : 512 * i + 128 * j + 128].astype(F32) for j in range(4)]
         ).astype(BF16)
-    pl.semaphore_wait(barrier, SLABS - 1 + 16 + 2)
+    pl.semaphore_wait(barrier, SLABS + 3)
     ex_q = Exchange(r.qsend, r.qrecv, r.ss_x.at[0], r.rs_x.at[0])
     ex_o = Exchange(r.osend, r.orecv, r.ss_x.at[1], r.rs_x.at[1])
     ex_g = Exchange(r.gsend, r.grecv, r.ss_x.at[2], r.rs_x.at[2])
     ex_d = Exchange(r.dsend, r.drecv, r.ss_x.at[3], r.rs_x.at[3])
-    ex_h = Exchange(r.hsend, r.hrecv, r.ss_x.at[4], r.rs_x.at[4], shared=4)
+    ex_h = Exchange(r.hsend, r.hline, r.ss_x.at[4], r.rs_x.at[4], parts=True)
     ex_p = Exchange(r.psend, r.precv, r.ss_x.at[5], r.rs_x.at[5])
     ex_q.start()
 
@@ -453,6 +457,13 @@
     residual = (r.flat[...] + nn(r.b_mixed[0:128, :], r.wo[...])).astype(BF16)
     normed_two, inverse_two = norm_stats(residual.astype(F32))
     r.b_h2[0:128, :] = (normed_two * gain_two).astype(BF16)
+    ex_h.wait()
+    h_at, h_copies = slab % 4, []
+    for n, (dz, dy) in enumerate(((1, 1), (0, 1), (1, 0))):
+        to = device(x, z + dz * (1 - 2 * (z % 2)), (y_hi + dy) % 2, y_lo, core)
+        h_copies.append(remote(r.hline.at[h_at], r.hline.at[h_at], r.ss_h.at[n], r.rs_h.at[n], to))
+    to_core_full(r.b_h2)
+    to_core_full(r.b_mixed)
     grad_hidden_two = jnp.zeros((128, 512), F32)
     for i in range(4):
         at = slice(512 * i, 512 * i + 512)
@@ -468,15 +479,13 @@
     r.grb[...] = r.gres[...].astype(BF16)
     r.gmix[...] = nt(r.grb[...], r.wo[...]).astype(BF16)
     r.gsend[...] = by_pair([r.gmix[:, 128 * j : 128 * j + 128].astype(F32) for j in range(4)]).astype(BF16)
-    ex_g.start()
     to_core_full(r.b_act)
     to_core_half(r.gu, r.b_gu)
-    to_core_full(r.b_h2)
-    to_core_full(r.b_mixed)
     to_core_half(r.grb, r.b_grb)
+    ex_g.start()
 
     one, two = Sum(r_one), Sum(r_two)
-    for copy in core_copies[1:5]:
+    for copy in core_copies[1:6]:
         copy.wait_recv()
     r.down32[...] = tn(r.b_act[...], r.b_cot[...]).reshape(SLABS, 32, 256)
     for i in range(2):
@@ -502,7 +511,7 @@
             r.gp[:, at] = back[i].astype(BF16)
     to_core_half(r.gp, r.b_gp)
 
-    for copy in core_copies[0:1] + core_copies[5:]:
+    for copy in core_copies[0:1] + core_copies[6:]:
         copy.wait_recv()
 
     def qkv_part(i):
@@ -511,6 +520,7 @@
     two.put(0, qkv_part(0), qkv_part(1))
     two.put(256, qkv_part(2), tn(r.b_mixed[...], r.b_grb[...]).reshape(SLABS, 8, 256))
     two.start()
+    one.middle()
 
     ex_g.wait()
     r.g32[...] = r.grecv[...].astype(F32).reshape(512, 128)
@@ -523,25 +533,21 @@
         for i in range(3):
             r.d32[i, pl.ds(j, 128, stride=4), :] = back[i]
 
-    ex_h.wait()
-    hidden_lines = r.hrecv[...].astype(F32).reshape(512, 512).astype(BF16)
-    for i in range(3):
-        r.psend[:, :, 128 * i : 128 * i + 128] = tn(hidden_lines, r.d32[i].astype(BF16)).reshape(SLABS, 8, 128).astype(BF16)
-    ex_p.start()
-    one.middle()
     for i in range(3):
         r.dsend[:, :, 128 * i : 128 * i + 128] = r.d32[i].reshape(SLABS, 8, 128).astype(BF16)
     ex_d.start()
     two.second()
     one.second()
-    ex_p.wait()
-    lines = jnp.sum(r.precv[...].astype(F32).reshape(16, 4, 8, 384), axis=0).astype(BF16)
-    case_at = y_lo * 2 + core
-    for i in range(3):
-        for j in range(4):
-            at = 512 * i + 128 * j
-            r.pgath[case_at, :, at : at + 128] = lines[j, :, 128 * i : 128 * i + 128]
-    p_copies = share(r.pgath, r.ss_p, r.rs_p)
+
+    for copy in h_copies:
+        copy.wait_recv()
+    line_grads = jnp.concatenate([r.d32[i].astype(BF16) for i in range(3)], axis=1)
+    for i in range(4):
+        hidden_lines = r.hline[i].astype(F32).reshape(512, 128).astype(BF16)
+        r.psend[16 * i : 16 * i + 16] = tn(hidden_lines, line_grads).reshape(16, 8, 384).astype(BF16)
+    ex_p.start()
+    two.along_z()
+    one.along_z()
 
     ex_d.wait()
     for i in range(3):
@@ -557,6 +563,15 @@
 
     two.gather()
     one.gather()
+    ex_p.wait()
+    lines = jnp.sum(r.precv[...].astype(F32).reshape(16, 4, 8, 384), axis=0).astype(BF16)
+    case_at = y_lo * 2 + core
+    for i in range(3):
+        for j in range(4):
+            at = 512 * i + 128 * j
+            r.pgath[case_at, :, at : at + 128] = lines[j, :, 128 * i : 128 * i + 128]
+    p_copies = share(r.pgath, r.ss_p, r.rs_p)
+
     own_rows = pl.ds(pl.multiple_of((slab // 2) * 16, 16), 16)
 
     def weight_rows(ref):
@@ -593,7 +608,7 @@
 
     for exchange in (ex_q, ex_o, ex_h, ex_g, ex_p, ex_d):
         exchange.drain()
-    for copy in core_copies + p_copies:
+    for copy in core_copies + h_copies + p_copies:
         copy.wait_send()
     one.drain()
     two.drain()

time: 93 us -> 86.8 us (0.933)
  Pallas kernels: 92.2 us -> 86.1 us
    pallas_call x1, Pallas kernels: 90.5 us -> 84.3 us  [body(): pl.pallas_call(functools.partial(kernel, factor, tree), out_shape=[jax.Sh...]
where the time goes in v5:
time: 86.8 us; the launch traced here: 86.7 us
  Pallas kernels  86.1 us (99%)
    pallas_call x1, Pallas kernels, body(): pl.pallas_call(functools.partial(kernel, factor, tree), out_shape=[jax.Sh...  84.3 us

profile of v5, /device:TPU:1, one launch (start us, length us, event | category | flops | bytes accessed | tf_op | source)
XLA Modules:
  0.0 86.7 jit_solution(7180095569308053712)
XLA Ops:
  0.6 84.3 %shard_map.135 = (bf16[2,8,8,512]{3,2,1,0:T(8,128)(2,1)}, f32[8,1536]{1,0:T(8,128)}, f32[8,512]{1,0:T(8,128)}, f32[8,2048]{1,0:T(8,128)}, f32[32,512]{1,0:T(8,128)}, /*index=5*/f32[8,128]{1,0:T(8,128)}, f32[8,128]{1,0:T(8,128)}) custom-call(bf16[2,8,8,512]{3,2,1,0:T(8,128)(2,1)} %bitcast.5, bf16[2,8,8,512]{3,2,1,0:T(8,128)(2,1)} %bitcast.6, ...), custom_call_target="tpu_custom_call" | custom-call | flops 3500000000 | bytes 7000000 | tf_op jit(solution)/shard_map/pallas_call | solution.py:633
  85.0 1.7 %shard_map.136 = (bf16[2,8,8,512]{3,2,1,0:T(8,128)(2,1)}, f32[8,1536]{1,0:T(8,128)}, f32[8,512]{1,0:T(8,128)}, f32[8,2048]{1,0:T(8,128)}, f32[32,512]{1,0:T(8,128)}, /*index=5*/f32[8]{0:T(128)}, f32[8]{0:T(128)}) custom-call(bf16[2,8,8,512]{3,2,1,0:T(8,128)(2,1)} %get-tuple-element.21.tok, f32[8,1536]{1,0:T(8,128)} %get-tuple-element.22.qkv, ...), custom_call_target="tpu_custom_call" | custom-call | tf_op jit(solution)/shard_map/pallas_call | solution.py:653

commit v6 on v5

--- a/solution.py
+++ b/solution.py
@@ -286,11 +286,8 @@
 
 
 class Exchange:
-    def __init__(self, send, recv, ss, rs, parts=False):
-        self.send, self.recv, self.ss, self.rs, self.parts = send, recv, ss, rs, parts
-
-    def landing(self, to):
-        return self.recv.at[to % 4] if self.parts else self.recv
+    def __init__(self, send, recv, ss, rs):
+        self.send, self.recv, self.ss, self.rs = send, recv, ss, rs
 
     def start(self):
         me = lax.axis_index("slab")
@@ -300,11 +297,11 @@
             kz, kx, ky = n // 8, (n // 2) % 4, n % 2
             dz, dx = far_first(kz, 4), far_first(kx, 2)
             to = device((x + dx) % 4, (z + dz) % 8, (y_hi + 1 - ky) % 2, y_lo, core)
-            remote(self.send.at[to[0]], self.landing(to[0]).at[me], self.ss, self.rs, to)
+            remote(self.send.at[to[0]], self.recv.at[me], self.ss, self.rs, to)
             return carry
 
         lax.fori_loop(0, SLABS - 1, one, 0)
-        self.landing(me)[me] = self.send[me]
+        self.recv[me] = self.send[me]
 
     def wait(self):
         got = self.send.at[pl.ds(0, SLABS - 1)]
@@ -324,15 +321,15 @@
     vm, dma = pltpu.VMEM, pltpu.SemaphoreType.DMA
     return dict(
         wq=vm((512, 1536), BF16), wo=vm((512, 512), BF16), wu=vm((512, 2048), BF16), wd=vm((2048, 512), BF16),
-        sw=dma((4,)),
+        sw=dma((8,)),
+        tok=vm((2, 8, 8, 512), BF16), cot_in=vm((2, 8, 8, 512), BF16), ga=vm((1, 512), F32), gm=vm((1, 512), F32),
         qkv=vm((128, 1536), BF16),
-        qsend=vm((SLABS, 8, 384), BF16), qrecv=vm((SLABS, 8, 384), BF16),
+        qsend=vm((SLABS, 8, 512), BF16), qrecv=vm((SLABS, 8, 512), BF16),
         osend=vm((SLABS, 8, 128), BF16), orecv=vm((SLABS, 8, 128), BF16),
         gsend=vm((SLABS, 8, 128), BF16), grecv=vm((SLABS, 8, 128), BF16),
         dsend=vm((SLABS, 8, 384), BF16), drecv=vm((SLABS, 8, 384), BF16),
-        hsend=vm((SLABS, 8, 128), BF16), hline=vm((4, SLABS, 8, 128), BF16), ss_h=dma((3,)), rs_h=dma((3,)),
-        psend=vm((SLABS, 8, 384), BF16), precv=vm((SLABS, 8, 384), BF16), pgath=vm((4, 8, 1536), BF16),
-        ss_x=dma((6,)), rs_x=dma((6,)), ss_p=dma((3,)), rs_p=dma((3,)),
+        hline=vm((4, SLABS, 8, 128), BF16), ss_h=dma((3,)), rs_h=dma((3,)),
+        ss_x=dma((4,)), rs_x=dma((4,)),
         z32=vm((3, 512, 128), F32), o32=vm((512, 128), F32), g32=vm((512, 128), F32), d32=vm((3, 512, 128), F32),
         px=vm((4, 128, 256), F32), py=vm((4, 128, 256), F32), pz=vm((4, 128, 256), F32),
         oxy=vm((128, 512), F32), dxy=vm((128, 1536), F32), gmix=vm((128, 512), BF16),
@@ -340,13 +337,14 @@
         b_h1=vm((256, 512), BF16), b_mixed=vm((256, 512), BF16), b_h2=vm((256, 512), BF16), b_act=vm((256, 2048), BF16),
         cot=vm((128, 512), BF16), gu=vm((128, 2048), BF16), grb=vm((128, 512), BF16), gp=vm((128, 1536), BF16),
         b_cot=vm((256, 256), BF16), b_gu=vm((256, 1024), BF16), b_grb=vm((256, 256), BF16), b_gp=vm((256, 768), BF16),
-        ss_core=dma((8,)), rs_core=dma((8,)),
-        down32=vm((SLABS, 32, 256), F32),
+        ss_core=dma((13,)), rs_core=dma((13,)),
+        zpart=vm((512, 384), F32), zpart_b=vm((512, 384), BF16), zpeer=vm((2, 512, 128), BF16),
+        down32=vm((SLABS, 32, 256), F32), out32=vm((512, 256), F32), qkv32=vm((512, 768), F32),
         one=sum_shapes(1024, True), two=sum_shapes(512, False),
     )
 
 
-def kernel(factor, tree, tok, cot, wq_h, wo_h, wu_h, wd_h, ga, gm, o_tok, o_qkv, o_out, o_up, o_down, o_g1, o_g2, *refs):
+def kernel(factor, tree, tok_h, cot_h, wq_h, wo_h, wu_h, wd_h, ga_h, gm_h, o_tok, o_qkv, o_out, o_up, o_down, o_g1, o_g2, *refs):
     r = jax.tree.unflatten(tree, refs)
     r, r_one, r_two = types.SimpleNamespace(**r), types.SimpleNamespace(**r["one"]), types.SimpleNamespace(**r["two"])
     x, z, y_hi, y_lo, core = places()
@@ -355,7 +353,9 @@
 
     loads = [
         pltpu.make_async_copy(src, dst, r.sw.at[n])
-        for n, (src, dst) in enumerate(((wq_h, r.wq), (wo_h, r.wo), (wd_h, r.wd), (wu_h, r.wu)))
+        for n, (src, dst) in enumerate(
+            ((tok_h, r.tok), (ga_h, r.ga), (wq_h, r.wq), (cot_h, r.cot_in), (gm_h, r.gm), (wd_h, r.wd), (wo_h, r.wo), (wu_h, r.wu))
+        )
     ]
     for load in loads:
         load.start()
@@ -375,14 +375,15 @@
     ):
         pl.semaphore_signal(barrier, inc=1, device_id=peer, device_id_type=MESH)
 
-    gain_one, gain_two = ga[...], gm[...]
-    r.flat[...] = to_rows(tok[...].astype(F32))
+    loads[0].wait()
+    loads[1].wait()
+    gain_one = r.ga[...]
+    r.flat[...] = to_rows(r.tok[...].astype(F32))
     normed_one, inverse_one = norm_stats(r.flat[...])
     hidden_one = normed_one * gain_one
     r.b_h1[0:128, :] = hidden_one.astype(BF16)
-    r.hsend[...] = by_pair([hidden_one[:, 128 * j : 128 * j + 128] for j in range(4)]).astype(BF16)
-    r.cot[...] = to_rows(cot[...].astype(F32)).astype(BF16)
-    loads[0].wait()
+    r.qsend[:, :, 384:512] = by_pair([hidden_one[:, 128 * j : 128 * j + 128] for j in range(4)]).astype(BF16)
+    loads[2].wait()
     for i in range(3):
         r.qkv[:, 512 * i : 512 * i + 512] = nn(r.b_h1[0:128, :], r.wq[:, 512 * i : 512 * i + 512]).astype(BF16)
     for i in range(3):
@@ -394,8 +395,6 @@
     ex_o = Exchange(r.osend, r.orecv, r.ss_x.at[1], r.rs_x.at[1])
     ex_g = Exchange(r.gsend, r.grecv, r.ss_x.at[2], r.rs_x.at[2])
     ex_d = Exchange(r.dsend, r.drecv, r.ss_x.at[3], r.rs_x.at[3])
-    ex_h = Exchange(r.hsend, r.hline, r.ss_x.at[4], r.rs_x.at[4], parts=True)
-    ex_p = Exchange(r.psend, r.precv, r.ss_x.at[5], r.rs_x.at[5])
     ex_q.start()
 
     core_copies = []
@@ -412,6 +411,10 @@
         core_copies.append(remote(theirs, dst.at[pl.ds(128, 128)], r.ss_core.at[n], r.rs_core.at[n], other))
         dst[0:128, :] = src[:, pl.ds(pl.multiple_of(core * half, 128), half)]
 
+    loads[3].wait()
+    loads[4].wait()
+    gain_two = r.gm[...]
+    r.cot[...] = to_rows(r.cot_in[...].astype(F32)).astype(BF16)
     to_core_full(r.b_h1)
     to_core_half(r.cot, r.b_cot)
 
@@ -426,7 +429,7 @@
         r.py[j] = line_probs(scores, mask_y)
         r.oxy[:, 128 * j : 128 * j + 128] = pair_out((r.px[j] + r.py[j]).astype(BF16), values)
 
-    loads[2].wait()
+    loads[5].wait()
     for i in range(4):
         at = slice(512 * i, 512 * i + 512)
         r.gact[:, at] = nt(r.cot[...], r.wd[at, :])
@@ -445,11 +448,15 @@
         r.o32[pl.ds(j, 128, stride=4), :] = pair_out(probs.astype(BF16), values)
     r.osend[...] = r.o32[...].reshape(SLABS, 8, 128).astype(BF16)
     ex_o.start()
-    ex_h.start()
-
-    loads[1].wait()
-    loads[3].wait()
+    r.hline[slab % 4] = r.qrecv[:, :, 384:512]
+
+    loads[6].wait()
+    loads[7].wait()
     ex_o.wait()
+    h_at, h_copies = slab % 4, []
+    for n, (dz, dy) in enumerate(((1, 1), (0, 1), (1, 0))):
+        to = device(x, z + dz * (1 - 2 * (z % 2)), (y_hi + dy) % 2, y_lo, core)
+        h_copies.append(remote(r.hline.at[h_at], r.hline.at[h_at], r.ss_h.at[n], r.rs_h.at[n], to))
     from_z = r.orecv[...].astype(F32).reshape(16, 4, 8, 128)
     for j in range(4):
         at = slice(128 * j, 128 * j + 128)
@@ -457,11 +464,6 @@
     residual = (r.flat[...] + nn(r.b_mixed[0:128, :], r.wo[...])).astype(BF16)
     normed_two, inverse_two = norm_stats(residual.astype(F32))
     r.b_h2[0:128, :] = (normed_two * gain_two).astype(BF16)
-    ex_h.wait()
-    h_at, h_copies = slab % 4, []
-    for n, (dz, dy) in enumerate(((1, 1), (0, 1), (1, 0))):
-        to = device(x, z + dz * (1 - 2 * (z % 2)), (y_hi + dy) % 2, y_lo, core)
-        h_copies.append(remote(r.hline.at[h_at], r.hline.at[h_at], r.ss_h.at[n], r.rs_h.at[n], to))
     to_core_full(r.b_h2)
     to_core_full(r.b_mixed)
     grad_hidden_two = jnp.zeros((128, 512), F32)
@@ -472,6 +474,8 @@
         tangent = jnp.tanh(ROOT * u * (1.0 + 0.044715 * square))
         half = 0.5 * (1.0 + tangent)
         r.b_act[0:128, at] = (u * half).astype(BF16)
+        act = r.b_act.at[:, at]
+        to_core_full(act)
         slope = half + 0.5 * u * (1.0 - tangent * tangent) * ROOT * (1.0 + 3.0 * 0.044715 * square)
         r.gu[:, at] = (r.gact[:, at] * slope).astype(BF16)
         grad_hidden_two = grad_hidden_two + nt(r.gu[:, at], r.wu[:, at])
@@ -479,13 +483,13 @@
     r.grb[...] = r.gres[...].astype(BF16)
     r.gmix[...] = nt(r.grb[...], r.wo[...]).astype(BF16)
     r.gsend[...] = by_pair([r.gmix[:, 128 * j : 128 * j + 128].astype(F32) for j in range(4)]).astype(BF16)
-    to_core_full(r.b_act)
     to_core_half(r.gu, r.b_gu)
     to_core_half(r.grb, r.b_grb)
+
     ex_g.start()
 
     one, two = Sum(r_one), Sum(r_two)
-    for copy in core_copies[1:6]:
+    for copy in core_copies[1:10]:
         copy.wait_recv()
     r.down32[...] = tn(r.b_act[...], r.b_cot[...]).reshape(SLABS, 32, 256)
     for i in range(2):
@@ -511,16 +515,12 @@
             r.gp[:, at] = back[i].astype(BF16)
     to_core_half(r.gp, r.b_gp)
 
-    for copy in core_copies[0:1] + core_copies[6:]:
+    r.out32[...] = tn(r.b_mixed[...], r.b_grb[...])
+    for copy in core_copies[0:1] + core_copies[10:]:
         copy.wait_recv()
-
-    def qkv_part(i):
-        return tn(r.b_h1[...], r.b_gp[:, 256 * i : 256 * i + 256]).reshape(SLABS, 8, 256)
-
-    two.put(0, qkv_part(0), qkv_part(1))
-    two.put(256, qkv_part(2), tn(r.b_mixed[...], r.b_grb[...]).reshape(SLABS, 8, 256))
-    two.start()
-    one.middle()
+    for i in range(3):
+        at = slice(256 * i, 256 * i + 256)
+        r.qkv32[:, at] = tn(r.b_h1[...], r.b_gp[:, at])
 
     ex_g.wait()
     r.g32[...] = r.grecv[...].astype(F32).reshape(512, 128)
@@ -533,21 +533,44 @@
         for i in range(3):
             r.d32[i, pl.ds(j, 128, stride=4), :] = back[i]
 
-    for i in range(3):
-        r.dsend[:, :, 128 * i : 128 * i + 128] = r.d32[i].reshape(SLABS, 8, 128).astype(BF16)
-    ex_d.start()
-    two.second()
-    one.second()
-
     for copy in h_copies:
         copy.wait_recv()
     line_grads = jnp.concatenate([r.d32[i].astype(BF16) for i in range(3)], axis=1)
     for i in range(4):
         hidden_lines = r.hline[i].astype(F32).reshape(512, 128).astype(BF16)
-        r.psend[16 * i : 16 * i + 16] = tn(hidden_lines, line_grads).reshape(16, 8, 384).astype(BF16)
-    ex_p.start()
+        r.zpart[128 * i : 128 * i + 128, :] = tn(hidden_lines, line_grads)
+    r.zpart_b[...] = r.zpart[...].astype(BF16)
+
+    def outer(owner):
+        return pl.ds(pl.multiple_of(owner * 256, 128), 128)
+
+    z_copies = [
+        remote(r.zpart_b.at[:, outer(1 - core)], r.zpeer.at[0], r.ss_core.at[11], r.rs_core.at[11], other),
+        remote(r.zpart_b.at[:, pl.ds(128, 128)], r.zpeer.at[1], r.ss_core.at[12], r.rs_core.at[12], other),
+    ]
+    one.middle()
+    pair_at = slab % 4
+    at_outer = pl.ds(pl.multiple_of(core * 256 + pair_at * 128, 128), 128)
+    at_keys = pl.ds(pl.multiple_of((1 - core) * 512 + (pair_at % 2) * 128, 128), 128)
+    owned = jnp.where(core == pair_at // 2, 1.0, 0.0)
+    z_copies[0].wait_recv()
+    r.qkv32[:, at_outer] = r.qkv32[:, at_outer] + (r.zpart[:, outer(core)] + r.zpeer[0].astype(F32))
+    z_copies[1].wait_recv()
+    r.qkv32[:, at_keys] = r.qkv32[:, at_keys] + owned * (r.zpart[:, 128:256] + r.zpeer[1].astype(F32))
+
+    def rows(ref, at):
+        return ref[:, at : at + 256].reshape(SLABS, 8, 256)
+
+    two.put(0, rows(r.qkv32, 0), rows(r.qkv32, 256))
+    two.put(256, rows(r.qkv32, 512), rows(r.out32, 0))
+    two.start()
+    for i in range(3):
+        r.dsend[:, :, 128 * i : 128 * i + 128] = r.d32[i].reshape(SLABS, 8, 128).astype(BF16)
+    one.second()
+    ex_d.start()
+    two.second()
+    one.along_z()
     two.along_z()
-    one.along_z()
 
     ex_d.wait()
     for i in range(3):
@@ -561,16 +584,8 @@
     o_tok[0] = first.astype(BF16)
     o_tok[1] = second.astype(BF16)
 
+    one.gather()
     two.gather()
-    one.gather()
-    ex_p.wait()
-    lines = jnp.sum(r.precv[...].astype(F32).reshape(16, 4, 8, 384), axis=0).astype(BF16)
-    case_at = y_lo * 2 + core
-    for i in range(3):
-        for j in range(4):
-            at = 512 * i + 128 * j
-            r.pgath[case_at, :, at : at + 128] = lines[j, :, 128 * i : 128 * i + 128]
-    p_copies = share(r.pgath, r.ss_p, r.rs_p)
 
     own_rows = pl.ds(pl.multiple_of((slab // 2) * 16, 16), 16)
 
@@ -595,20 +610,17 @@
         return jnp.broadcast_to(jnp.sum(rows, axis=1, keepdims=True) / own, (8, 128))
 
     o_g2[...] = over_gain(o_up[...] * weight_rows(r.wu), gain_two)
-    for copy in p_copies:
-        copy.wait_recv()
-    o_qkv[...] = jnp.sum(r.pgath[...].astype(F32), axis=0) * factor
     for c, full in enumerate(two.finish()):
         full = full * factor
-        o_qkv[:, 768 * c : 768 * c + 256] += full[0:8, 0:256]
-        o_qkv[:, 768 * c + 256 : 768 * c + 512] += full[8:16, 0:256]
-        o_qkv[:, 768 * c + 512 : 768 * c + 768] += full[0:8, 256:512]
+        o_qkv[:, 768 * c : 768 * c + 256] = full[0:8, 0:256]
+        o_qkv[:, 768 * c + 256 : 768 * c + 512] = full[8:16, 0:256]
+        o_qkv[:, 768 * c + 512 : 768 * c + 768] = full[0:8, 256:512]
         o_out[:, 256 * c : 256 * c + 256] = full[8:16, 256:512]
     o_g1[...] = over_gain(o_qkv[...] * weight_rows(r.wq), gain_one)
 
-    for exchange in (ex_q, ex_o, ex_h, ex_g, ex_p, ex_d):
+    for exchange in (ex_q, ex_o, ex_g, ex_d):
         exchange.drain()
-    for copy in core_copies + h_copies + p_copies:
+    for copy in core_copies + h_copies + z_copies:
         copy.wait_send()
     one.drain()
     two.drain()
@@ -633,7 +645,7 @@
     result = pl.pallas_call(
         functools.partial(kernel, factor, tree),
         out_shape=[jax.ShapeDtypeStruct((2, 8, 8, width), BF16)] + [jax.ShapeDtypeStruct(s, F32) for s in outs],
-        in_specs=[vmem, vmem] + [any_space] * 4 + [vmem, vmem],
+        in_specs=[any_space] * 8,
         out_specs=[vmem] * 7,
         scratch_shapes=leaves,
         compiler_params=pltpu.CompilerParams(

time: 86.8 us -> 81.7 us (0.941)
  Pallas kernels: 86.1 us -> 81 us
    pallas_call x1, Pallas kernels: 84.3 us -> 79.3 us  [body(): pl.pallas_call(functools.partial(kernel, factor, tree), out_shape=[jax.Sh...]
where the time goes in v6:
time: 81.7 us; the launch traced here: 81.6 us
  Pallas kernels  81 us (99%)
    pallas_call x1, Pallas kernels, body(): pl.pallas_call(functools.partial(kernel, factor, tree), out_shape=[jax.Sh...  79.3 us
    pallas_call x1, Pallas kernels, body(): pl.pallas_call(results_kernel, out_shape=[jax.ShapeDtypeStruct((2, 8, 8,...  1.72 us

profile of v6, /device:TPU:1, one launch (start us, length us, event | category | flops | bytes accessed | tf_op | source)
XLA Modules:
  0.0 81.6 jit_solution(6190766802702506573)
XLA Ops:
  0.6 79.3 %shard_map.135 = (bf16[2,8,8,512]{3,2,1,0:T(8,128)(2,1)}, f32[8,1536]{1,0:T(8,128)}, f32[8,512]{1,0:T(8,128)}, f32[8,2048]{1,0:T(8,128)}, f32[32,512]{1,0:T(8,128)}, /*index=5*/f32[8,128]{1,0:T(8,128)}, f32[8,128]{1,0:T(8,128)}) custom-call(bf16[2,8,8,512]{3,2,1,0:T(8,128)(2,1)} %bitcast.5, bf16[2,8,8,512]{3,2,1,0:T(8,128)(2,1)} %bitcast.6, ...), custom_call_target="tpu_custom_call" | custom-call | flops 3500000000 | bytes 7000000 | tf_op jit(solution)/shard_map/pallas_call | solution.py:645
  79.9 1.7 %shard_map.136 = (bf16[2,8,8,512]{3,2,1,0:T(8,128)(2,1)}, f32[8,1536]{1,0:T(8,128)}, f32[8,512]{1,0:T(8,128)}, f32[8,2048]{1,0:T(8,128)}, f32[32,512]{1,0:T(8,128)}, /*index=5*/f32[8]{0:T(128)}, f32[8]{0:T(128)}) custom-call(bf16[2,8,8,512]{3,2,1,0:T(8,128)(2,1)} %get-tuple-element.21.tok, f32[8,1536]{1,0:T(8,128)} %get-tuple-element.22.qkv, ...), custom_call_target="tpu_custom_call" | custom-call | tf_op jit(solution)/shard_map/pallas_call | solution.py:665

commit v7 on v6

--- a/solution.py
+++ b/solution.py
@@ -324,12 +324,13 @@
         sw=dma((8,)),
         tok=vm((2, 8, 8, 512), BF16), cot_in=vm((2, 8, 8, 512), BF16), ga=vm((1, 512), F32), gm=vm((1, 512), F32),
         qkv=vm((128, 1536), BF16),
-        qsend=vm((SLABS, 8, 512), BF16), qrecv=vm((SLABS, 8, 512), BF16),
+        qsend=vm((SLABS, 8, 384), BF16), qrecv=vm((SLABS, 8, 384), BF16),
+        hsend=vm((SLABS, 8, 128), BF16), hrecv=vm((SLABS, 8, 128), BF16),
         osend=vm((SLABS, 8, 128), BF16), orecv=vm((SLABS, 8, 128), BF16),
         gsend=vm((SLABS, 8, 128), BF16), grecv=vm((SLABS, 8, 128), BF16),
         dsend=vm((SLABS, 8, 384), BF16), drecv=vm((SLABS, 8, 384), BF16),
         hline=vm((4, SLABS, 8, 128), BF16), ss_h=dma((3,)), rs_h=dma((3,)),
-        ss_x=dma((4,)), rs_x=dma((4,)),
+        ss_x=dma((5,)), rs_x=dma((5,)),
         z32=vm((3, 512, 128), F32), o32=vm((512, 128), F32), g32=vm((512, 128), F32), d32=vm((3, 512, 128), F32),
         px=vm((4, 128, 256), F32), py=vm((4, 128, 256), F32), pz=vm((4, 128, 256), F32),
         oxy=vm((128, 512), F32), dxy=vm((128, 1536), F32), gmix=vm((128, 512), BF16),
@@ -357,7 +358,7 @@
             ((tok_h, r.tok), (ga_h, r.ga), (wq_h, r.wq), (cot_h, r.cot_in), (gm_h, r.gm), (wd_h, r.wd), (wo_h, r.wo), (wu_h, r.wu))
         )
     ]
-    for load in loads:
+    for load in loads[0:5]:
         load.start()
 
     barrier = pltpu.get_barrier_semaphore()
@@ -382,7 +383,7 @@
     normed_one, inverse_one = norm_stats(r.flat[...])
     hidden_one = normed_one * gain_one
     r.b_h1[0:128, :] = hidden_one.astype(BF16)
-    r.qsend[:, :, 384:512] = by_pair([hidden_one[:, 128 * j : 128 * j + 128] for j in range(4)]).astype(BF16)
+    r.hsend[...] = by_pair([hidden_one[:, 128 * j : 128 * j + 128] for j in range(4)]).astype(BF16)
     loads[2].wait()
     for i in range(3):
         r.qkv[:, 512 * i : 512 * i + 512] = nn(r.b_h1[0:128, :], r.wq[:, 512 * i : 512 * i + 512]).astype(BF16)
@@ -390,12 +391,16 @@
         r.qsend[:, :, 128 * i : 128 * i + 128] = by_pair(
             [r.qkv[:, 512 * i + 128 * j : 512 * i + 128 * j + 128].astype(F32) for j in range(4)]
         ).astype(BF16)
+    for load in loads[5:]:
+        load.start()
     pl.semaphore_wait(barrier, SLABS + 3)
     ex_q = Exchange(r.qsend, r.qrecv, r.ss_x.at[0], r.rs_x.at[0])
     ex_o = Exchange(r.osend, r.orecv, r.ss_x.at[1], r.rs_x.at[1])
     ex_g = Exchange(r.gsend, r.grecv, r.ss_x.at[2], r.rs_x.at[2])
     ex_d = Exchange(r.dsend, r.drecv, r.ss_x.at[3], r.rs_x.at[3])
+    ex_h = Exchange(r.hsend, r.hrecv, r.ss_x.at[4], r.rs_x.at[4])
     ex_q.start()
+    ex_h.start()
 
     core_copies = []
 
@@ -448,7 +453,8 @@
         r.o32[pl.ds(j, 128, stride=4), :] = pair_out(probs.astype(BF16), values)
     r.osend[...] = r.o32[...].reshape(SLABS, 8, 128).astype(BF16)
     ex_o.start()
-    r.hline[slab % 4] = r.qrecv[:, :, 384:512]
+    ex_h.wait()
+    r.hline[slab % 4] = r.hrecv[...]
 
     loads[6].wait()
     loads[7].wait()
@@ -618,7 +624,7 @@
         o_out[:, 256 * c : 256 * c + 256] = full[8:16, 256:512]
     o_g1[...] = over_gain(o_qkv[...] * weight_rows(r.wq), gain_one)
 
-    for exchange in (ex_q, ex_o, ex_g, ex_d):
+    for exchange in (ex_q, ex_h, ex_o, ex_g, ex_d):
         exchange.drain()
     for copy in core_copies + h_copies + z_copies:
         copy.wait_send()

time: 81.7 us -> 78.9 us (0.966)
  Pallas kernels: 81 us -> 78.1 us
    pallas_call x1, Pallas kernels: 79.3 us -> 76.4 us  [body(): pl.pallas_call(functools.partial(kernel, factor, tree), out_shape=[jax.Sh...]
where the time goes in v7:
time: 78.9 us; the launch traced here: 78.8 us
  Pallas kernels  78.1 us (99%)
    pallas_call x1, Pallas kernels, body(): pl.pallas_call(functools.partial(kernel, factor, tree), out_shape=[jax.Sh...  76.4 us
    pallas_call x1, Pallas kernels, body(): pl.pallas_call(results_kernel, out_shape=[jax.ShapeDtypeStruct((2, 8, 8,...  1.72 us

profile of v7, /device:TPU:1, one launch (start us, length us, event | category | flops | bytes accessed | tf_op | source)
XLA Modules:
  0.0 78.8 jit_solution(11358395899566698225)
XLA Ops:
  0.6 76.4 %shard_map.135 = (bf16[2,8,8,512]{3,2,1,0:T(8,128)(2,1)}, f32[8,1536]{1,0:T(8,128)}, f32[8,512]{1,0:T(8,128)}, f32[8,2048]{1,0:T(8,128)}, f32[32,512]{1,0:T(8,128)}, /*index=5*/f32[8,128]{1,0:T(8,128)}, f32[8,128]{1,0:T(8,128)}) custom-call(bf16[2,8,8,512]{3,2,1,0:T(8,128)(2,1)} %bitcast.5, bf16[2,8,8,512]{3,2,1,0:T(8,128)(2,1)} %bitcast.6, ...), custom_call_target="tpu_custom_call" | custom-call | flops 3500000000 | bytes 7000000 | tf_op jit(solution)/shard_map/pallas_call | solution.py:651
  77.1 1.7 %shard_map.136 = (bf16[2,8,8,512]{3,2,1,0:T(8,128)(2,1)}, f32[8,1536]{1,0:T(8,128)}, f32[8,512]{1,0:T(8,128)}, f32[8,2048]{1,0:T(8,128)}, f32[32,512]{1,0:T(8,128)}, /*index=5*/f32[8]{0:T(128)}, f32[8]{0:T(128)}) custom-call(bf16[2,8,8,512]{3,2,1,0:T(8,128)(2,1)} %get-tuple-element.21.tok, f32[8,1536]{1,0:T(8,128)} %get-tuple-element.22.qkv, ...), custom_call_target="tpu_custom_call" | custom-call | tf_op jit(solution)/shard_map/pallas_call | solution.py:671

commit v8 on v7

--- a/solution.py
+++ b/solution.py
@@ -341,7 +341,7 @@
         ss_core=dma((13,)), rs_core=dma((13,)),
         zpart=vm((512, 384), F32), zpart_b=vm((512, 384), BF16), zpeer=vm((2, 512, 128), BF16),
         down32=vm((SLABS, 32, 256), F32), out32=vm((512, 256), F32), qkv32=vm((512, 768), F32),
-        one=sum_shapes(1024, True), two=sum_shapes(512, False),
+        one=sum_shapes(1024, True), two=sum_shapes(512, True),
     )
 
 
@@ -573,6 +573,7 @@
     for i in range(3):
         r.dsend[:, :, 128 * i : 128 * i + 128] = r.d32[i].reshape(SLABS, 8, 128).astype(BF16)
     one.second()
+    two.middle()
     ex_d.start()
     two.second()
     one.along_z()

time: 78.9 us -> 78.2 us (level)
  no operation moved by 1% of the time
where the time goes in v8:
time: 78.2 us; the launch traced here: 78 us
  Pallas kernels  77.4 us (99%)
    pallas_call x1, Pallas kernels, body(): pl.pallas_call(functools.partial(kernel, factor, tree), out_shape=[jax.Sh...  75.7 us
    pallas_call x1, Pallas kernels, body(): pl.pallas_call(results_kernel, out_shape=[jax.ShapeDtypeStruct((2, 8, 8,...  1.72 us

profile of v8, /device:TPU:1, one launch (start us, length us, event | category | flops | bytes accessed | tf_op | source)
XLA Modules:
  0.0 78.0 jit_solution(5792730938827165379)
XLA Ops:
  0.6 75.7 %shard_map.135 = (bf16[2,8,8,512]{3,2,1,0:T(8,128)(2,1)}, f32[8,1536]{1,0:T(8,128)}, f32[8,512]{1,0:T(8,128)}, f32[8,2048]{1,0:T(8,128)}, f32[32,512]{1,0:T(8,128)}, /*index=5*/f32[8,128]{1,0:T(8,128)}, f32[8,128]{1,0:T(8,128)}) custom-call(bf16[2,8,8,512]{3,2,1,0:T(8,128)(2,1)} %bitcast.5, bf16[2,8,8,512]{3,2,1,0:T(8,128)(2,1)} %bitcast.6, ...), custom_call_target="tpu_custom_call" | custom-call | flops 3500000000 | bytes 7000000 | tf_op jit(solution)/shard_map/pallas_call | solution.py:652
  76.3 1.7 %shard_map.136 = (bf16[2,8,8,512]{3,2,1,0:T(8,128)(2,1)}, f32[8,1536]{1,0:T(8,128)}, f32[8,512]{1,0:T(8,128)}, f32[8,2048]{1,0:T(8,128)}, f32[32,512]{1,0:T(8,128)}, /*index=5*/f32[8]{0:T(128)}, f32[8]{0:T(128)}) custom-call(bf16[2,8,8,512]{3,2,1,0:T(8,128)(2,1)} %get-tuple-element.21.tok, f32[8,1536]{1,0:T(8,128)} %get-tuple-element.22.qkv, ...), custom_call_target="tpu_custom_call" | custom-call | tf_op jit(solution)/shard_map/pallas_call | solution.py:672
